TPU v7x, 32 devices: a whole 2x2x4 slice. The times are simulated.
32 devices in a mesh: groups: 2 (over y), leaf: 4 (over z), near: 2 (over x), rhs: 2 (over core).
Axes of the slice: x: 2, y: 2, z: 4, core: 2. Of those that a mesh axis runs over, the one named last changes fastest.
Arguments:
- points: bfloat16 [3, 256, 1024], P(None, None, ('groups', 'leaf')), parts along dimension 2, may hold values from -24 to 24, as said below
- charges: bfloat16 [256, 64, 1024], P('near', 'rhs', ('groups', 'leaf')), parts along dimension 2, may hold values from -6 to 6
- basis: bfloat16 [256, 64, 1024], P('near', None, ('groups', 'leaf')), parts along dimension 2, may hold values from -0.375 to 0.375
- transfer: bfloat16 [64, 64, 1024], P(None, None, ('groups', 'leaf')), parts along dimension 2, may hold values from -0.25 to 0.25
- leaf_skeleton: bfloat16 [3, 64, 1024], P(None, None, ('groups', 'leaf')), parts along dimension 2, may hold values from -2 to 2
- parent_skeleton: bfloat16 [3, 64, 128], P(None, None, ('groups', 'leaf')), parts along dimension 2, may hold values from -2 to 2
- near_list: int32 [25, 1024], P(None, ('groups', 'leaf')), parts along dimension 1, may hold values from 0 to 511, as said below
- near_count: int32 [1024], P(('groups', 'leaf')), parts along dimension 0, may hold values from 1 to 25
- leaf_far: int32 [16, 1024], P(None, ('groups', 'leaf')), parts along dimension 1, may hold values from 0 to 511, as said below
- parent_far: int32 [16, 128], P(None, ('groups', 'leaf')), parts along dimension 1, may hold values from 0 to 63, as said below
Outputs:
- potential: bfloat16 [256, 64, 1024], P('near', 'rhs', ('groups', 'leaf')), parts along dimension 2
There are 2 independent parts, one for each index of `groups`. A program takes and returns all parts, laid end to end along the dimension named above; each array names one. Nothing has to cross between parts.
Inputs may be any that keep to these rules, and one draw needn't show every extreme that they name: `points`: offsets of an element from its leaf's centre; the third component lies within 2 of zero. `near_list`: slot 0 of leaf i is i; the other live slots name distinct leaves whose strip positions (i mod 8, floor(i / 8)) differ from i's by at most 2 in each coordinate; slots from near_count[i] on hold i. `leaf_far`: entry of leaf i names a leaf that is not in i's 5 by 5 near block and whose strip row floor(j / 8) differs from i's by at most 5; the same strip row occurs only where the strip positions j mod 8 and i mod 8 differ by more than 2; entries may repeat. `parent_far`: entry of parent p names a parent q with |q - p| >= 6; entries may repeat.
All inputs are finite; a program needn't handle non-finite values.
Results may differ from a plain program's by a relative error of at most 0.0058.
Values may be sent and summed in bfloat16 or wider, within the bound.
A program may use at most 64 MiB of HBM per device.

v0:
```python
import jax
import jax.numpy as jnp
from jax import lax
from jax.sharding import PartitionSpec as P

STRIP = 8


near_scale = 0.25
coupling_scale = 0.0625
softening = 0.25
spacing = 16.0


def padded(cells, sides, width):
    for axis, dim in sides:
        count = lax.axis_size(axis)
        ends = count - 1
        head = lax.slice_in_dim(cells, 0, width, axis=dim)
        tail = lax.slice_in_dim(cells, cells.shape[dim] - width, cells.shape[dim], axis=dim)
        cells = jnp.concatenate(
            [
                lax.ppermute(tail, axis, [(i, (i + 1) % count) for i in range(ends)]),
                cells,
                lax.ppermute(head, axis, [((i + 1) % count, i) for i in range(ends)]),
            ],
            axis=dim,
        )
    return cells


def element_kernel(row_points, row_ids, col_points, col_ids):
    shift_x = (row_ids % STRIP - col_ids % STRIP).astype(jnp.float32) * spacing
    shift_y = (row_ids // STRIP - col_ids // STRIP).astype(jnp.float32) * spacing
    shifts = (shift_x, shift_y, jnp.zeros_like(shift_x))
    running = jnp.zeros((row_points.shape[1], col_points.shape[1], row_ids.shape[0]), jnp.float32)
    for component in range(3):
        offset_gap = (
            row_points[component].astype(jnp.float32)[:, None, :]
            - col_points[component].astype(jnp.float32)[None, :, :]
        )
        offset_gap = offset_gap + shifts[component][None, None, :]
        running = running + offset_gap * offset_gap
    return near_scale / jnp.sqrt(running + softening)


def skeleton_kernel(targets, sources):
    running = jnp.zeros((targets.shape[1], sources.shape[1], targets.shape[2]), jnp.float32)
    for component in range(3):
        offset_gap = (
            targets[component].astype(jnp.float32)[:, None, :]
            - sources[component].astype(jnp.float32)[None, :, :]
        )
        running = running + offset_gap * offset_gap
    return coupling_scale / jnp.sqrt(running + softening)


def coupling_field(targets, source_points, source_moments, far_ids):

    def far_step(position, running):
        source_ids = lax.dynamic_index_in_dim(far_ids, position, 0, keepdims=False)
        far_tile = skeleton_kernel(targets, jnp.take(source_points, source_ids, axis=2)).astype(
            jnp.bfloat16
        )
        sources = jnp.take(source_moments, source_ids, axis=2)
        return running + jnp.einsum(
            "abi,bci->aci", far_tile, sources, preferred_element_type=jnp.float32
        )

    initial = jnp.zeros((targets.shape[1], source_moments.shape[1], far_ids.shape[1]), jnp.float32)
    return lax.fori_loop(0, far_ids.shape[0], far_step, initial)


def per_device(
    points,
    charges,
    basis,
    transfer,
    leaf_skeleton,
    parent_skeleton,
    near_list,
    near_count,
    leaf_far,
    parent_far,
):
    rows_here = charges.shape[0]
    columns = charges.shape[1]
    leaf_count = charges.shape[2]
    rank_size = basis.shape[1]
    near_index = lax.axis_index("near")
    leaf_index = lax.axis_index("leaf")
    near_parts = lax.axis_size("near")
    near_reach = 2 * STRIP + 2
    far_reach = 6 * STRIP - 1
    thin_charges, border_points = (
        padded(charges, (("leaf", 2),), near_reach),
        padded(points, (("leaf", 2),), near_reach),
    )
    border_charges = lax.all_gather(thin_charges, "near", axis=0, tiled=True)
    first_leaf = leaf_index * leaf_count
    row_ids = first_leaf + jnp.arange(leaf_count, dtype=jnp.int32)
    own_points = lax.dynamic_slice_in_dim(points, near_index * rows_here, rows_here, 1)

    def near_step(position, running):
        source_ids = lax.dynamic_index_in_dim(near_list, position, 0, keepdims=False)
        local_ids = source_ids - (first_leaf - near_reach)
        near_tile = element_kernel(
            own_points, row_ids, jnp.take(border_points, local_ids, axis=2), source_ids
        )
        near_tile = jnp.where((position < near_count)[None, None, :], near_tile, 0.0).astype(
            jnp.bfloat16
        )
        sources = jnp.take(border_charges, local_ids, axis=2)
        return running + jnp.einsum(
            "rsi,sci->rci", near_tile, sources, preferred_element_type=jnp.float32
        )

    initial = jnp.zeros((rows_here, columns, leaf_count), jnp.float32)
    near_part = lax.fori_loop(0, near_list.shape[0], near_step, initial)
    partial_moments = jnp.einsum("sai,sci->aci", basis, charges, preferred_element_type=jnp.float32)
    moments0 = lax.psum(partial_moments, "near").astype(jnp.bfloat16)
    lifted = jnp.einsum("abi,aci->bci", transfer, moments0, preferred_element_type=jnp.float32)
    moments1 = (
        lifted.reshape(rank_size, columns, leaf_count // STRIP, STRIP)
        .sum(axis=3)
        .astype(jnp.bfloat16)
    )
    border_moments, border_skeleton = (
        padded(moments0, (("leaf", 2),), far_reach),
        padded(leaf_skeleton, (("leaf", 2),), far_reach),
    )
    every_moments, every_skeleton = (
        lax.all_gather(moments1, "leaf", axis=2, tiled=True),
        lax.all_gather(parent_skeleton, "leaf", axis=2, tiled=True),
    )
    local_far = leaf_far - (first_leaf - far_reach)
    share_leaf = leaf_far.shape[0] // near_parts
    share_parent = parent_far.shape[0] // near_parts
    own_leaf_slots = lax.dynamic_slice_in_dim(local_far, near_index * share_leaf, share_leaf, 0)
    own_parent_slots = lax.dynamic_slice_in_dim(
        parent_far, near_index * share_parent, share_parent, 0
    )
    field0 = coupling_field(leaf_skeleton, border_skeleton, border_moments, own_leaf_slots)
    field1 = coupling_field(parent_skeleton, every_skeleton, every_moments, own_parent_slots)
    field0, field1 = lax.psum((field0, field1), "near")
    parent_field = field1.astype(jnp.bfloat16)
    spread = jnp.broadcast_to(parent_field[:, :, :, None], parent_field.shape + (STRIP,)).reshape(
        rank_size, columns, leaf_count
    )
    leaf_field = (
        field0 + jnp.einsum("abi,bci->aci", transfer, spread, preferred_element_type=jnp.float32)
    ).astype(jnp.bfloat16)
    far_part = jnp.einsum("sai,aci->sci", basis, leaf_field, preferred_element_type=jnp.float32)
    return (near_part + far_part).astype(jnp.bfloat16)


def solution(mesh):
    placed = (
        P(None, None, ("groups", "leaf")),
        P("near", "rhs", ("groups", "leaf")),
        P("near", None, ("groups", "leaf")),
        P(None, None, ("groups", "leaf")),
        P(None, None, ("groups", "leaf")),
        P(None, None, ("groups", "leaf")),
        P(None, ("groups", "leaf")),
        P(("groups", "leaf")),
        P(None, ("groups", "leaf")),
        P(None, ("groups", "leaf")),
    )
    return jax.shard_map(
        per_device,
        mesh=mesh,
        in_specs=placed,
        out_specs=P("near", "rhs", ("groups", "leaf")),
        check_vma=False,
    )
```

profile of v0, /device:TPU:13, one launch (start us, length us, event | category | flops | bytes accessed | tf_op | source)
XLA Modules:
  0.0 744.1 jit_solution(15621096976699468625)
XLA Ops:
  9.1 4.2 copy.59
  15.8 51.9 %all-reduce.5 = bf16[64,32,128]{0,1,2:T(8,128)(2,1)S(1)} all-reduce(f32[64,32,128]{0,1,2:T(8,128)} %convolution_bitcast_fusion.1), channel_id=1, replica_groups=mesh['groups'=2,'leaf'=4,'near'=2,'rhs'=2] {'near'}, use_global_device_ids=true, to_apply=%region_2.3 | all-reduce | flops 262144 | bytes 1572864 | tf_op jit(solution)/shard_map/psum | solution.py:121
  68.7 3.2 collective-permute-start.4
  88.3 100.6 %while.48 = (s32[]{:T(128)}, f32[64,32,128]{0,1,2:T(8,128)}, s32[8,128]{1,0:T(8,128)S(1)}, bf16[64,32,222]{0,1,2:T(8,128)(2,1)}, bf16[3,64,128]{1,2,0:T(8,128)(2...) while((s32[]{:T(128)}, f32[64,32,128]{0,1,2:T(8,128)}, s32[8,128]{1,0:T(8,128)S(1)}, ...), condition=%wide.region_4.5_spmd.clone, body=%wide.region_3.4_spmd.clone.sunk | while | flops 40183936 | bytes 4365799 | solution.py:71
  94.2 6.3 bitcast_add_fusion.6
  106.4 6.7 bitcast_add_fusion.6
  119.1 6.7 bitcast_add_fusion.6
  131.7 6.7 bitcast_add_fusion.6
  144.3 6.7 bitcast_add_fusion.6
  153.1 3.2 gather_fusion.1
  157.0 6.7 bitcast_add_fusion.6
  169.6 6.7 bitcast_add_fusion.6
  182.2 6.7 bitcast_add_fusion.6
  190.7 3.4 collective-permute-start
  201.3 3.2 collective-permute-start.3
  204.5 4.8 copy.62
  211.5 12.2 %all_gather.10 = bf16[64,32,64]{0,1,2:T(8,128)(2,1)S(1)} all-gather(bf16[64,32,16]{0,1,2:T(8,128)(2,1)S(1)} %bitcast_reduce_fusion), channel_id=1, replica_groups=mesh['groups'=2,'leaf'=4,'near'=2,'rhs'=2] {'leaf'}, dimensions={2}, use_global_device_ids=true | all-gather | bytes 327680 | tf_op jit(solution)/shard_map/all_gather | solution.py:133
  223.8 11.2 %all_gather.11 = bf16[3,64,64]{1,2,0:T(8,128)(2,1)S(1)} all-gather(bf16[3,64,16]{1,2,0:T(8,128)(2,1)S(1)} %copy-done.5), channel_id=1, replica_groups=mesh['groups'=2,'leaf'=4,'near'=2,'rhs'=2] {'leaf'}, dimensions={2}, use_global_device_ids=true | all-gather | bytes 30720 | tf_op jit(solution)/shard_map/all_gather | solution.py:134
  237.7 17.7 %while.49 = (s32[]{:T(128)}, f32[64,32,16]{0,1,2:T(8,128)S(1)}, s32[8,16]{1,0:T(8,128)S(1)}, bf16[64,32,64]{0,1,2:T(8,128)(2,1)S(1)}, bf16[3,64,16]{1,2,0:T(8,12...) while((s32[]{:T(128)}, f32[64,32,16]{0,1,2:T(8,128)S(1)}, ...), condition=%wide.region_8.9_spmd.clone, body=%wide.region_7.8_spmd.clone.sunk | while | flops 5023891 | bytes 549399 | solution.py:71
  255.4 8.4 %all-reduce.6 = bf16[64,32,16]{0,1,2:T(8,128)(2,1)S(1)} all-reduce(f32[64,32,16]{0,1,2:T(8,128)S(1)} %get-tuple-element.552), channel_id=1, replica_groups=mesh['groups'=2,'leaf'=4,'near'=2,'rhs'=2] {'near'}, use_global_device_ids=true, to_apply=%region_9.10 | all-reduce | flops 32768 | bytes 196608 | tf_op jit(solution)/shard_map/psum | solution.py:145
  267.1 5.4 fusion.62
  272.5 25.6 %all-gather.2.cloned.1.call-done = bf16[256,32,164]{0,1,2:T(8,128)(2,1)} async-done(((bf16[128,32,164]{0,1,2:T(8,128)(2,1)}), bf16[256,32,164]{0,1,2:T(8,128)(2,1)}) %all-gather.2.cloned.1.call-update) | async-done | bytes 2686992 | tf_op jit(solution)/shard_map/all_gather | solution.py:99
  298.1 434.2 %while.50 = (s32[]{:T(128)}, f32[128,32,128]{0,1,2:T(8,128)}, s32[25,128]{1,0:T(8,128)}, s32[]{:T(128)}, bf16[256,32,164]{0,1,2:T(8,128)(2,1)}, /*index=5*/s32[1...) while((s32[]{:T(128)}, f32[128,32,128]{0,1,2:T(8,128)}, ...), condition=%wide.region_1.2_spmd.clone.clone.clone, body=%wide.region_0.1_spmd.clone.clone.clone.sunk | while | flops 329508992 | bytes 18132780 | solution.py:119
  304.4 11.0 %bitcast_add_fusion.7 = f32[128,32,128]{0,1,2:T(8,128)} fusion(f32[128,32,128]{0,1,2:T(8,128)} %get-tuple-element.974, f32[256,128]{0,1:T(8,128)S(1)} %bitcast.219, f32[128,128]{0,1:T(8,128)S(1)} %get-tuple-element.955, f32[128]{0:T(128)S(1)} %convert_multiply_fusion.2, f32[256,128]{0,1:T(8,128)S(1)} %bitcast.220, ...), kind=kOutput, calls=%fused_computation.75.clone.3 | convolution fusion | flops 328204288 | bytes 6882433 | tf_op jit(solution)/shard_map/while/body/eval_jaxpr/rsi,sci->rci/dot_general | solution.py:114
  321.7 11.1 %bitcast_add_fusion.7 = f32[128,32,128]{0,1,2:T(8,128)} fusion(f32[128,32,128]{0,1,2:T(8,128)} %get-tuple-element.974, f32[256,128]{0,1:T(8,128)S(1)} %bitcast.219, f32[128,128]{0,1:T(8,128)S(1)} %get-tuple-element.955, f32[128]{0:T(128)S(1)} %convert_multiply_fusion.2, f32[256,128]{0,1:T(8,128)S(1)} %bitcast.220, ...), kind=kOutput, calls=%fused_computation.75.clone.3 | convolution fusion | flops 328204288 | bytes 6882433 | tf_op jit(solution)/shard_map/while/body/eval_jaxpr/rsi,sci->rci/dot_general | solution.py:114
  339.1 11.1 %bitcast_add_fusion.7 = f32[128,32,128]{0,1,2:T(8,128)} fusion(f32[128,32,128]{0,1,2:T(8,128)} %get-tuple-element.974, f32[256,128]{0,1:T(8,128)S(1)} %bitcast.219, f32[128,128]{0,1:T(8,128)S(1)} %get-tuple-element.955, f32[128]{0:T(128)S(1)} %convert_multiply_fusion.2, f32[256,128]{0,1:T(8,128)S(1)} %bitcast.220, ...), kind=kOutput, calls=%fused_computation.75.clone.3 | convolution fusion | flops 328204288 | bytes 6882433 | tf_op jit(solution)/shard_map/while/body/eval_jaxpr/rsi,sci->rci/dot_general | solution.py:114
  356.5 11.1 %bitcast_add_fusion.7 = f32[128,32,128]{0,1,2:T(8,128)} fusion(f32[128,32,128]{0,1,2:T(8,128)} %get-tuple-element.974, f32[256,128]{0,1:T(8,128)S(1)} %bitcast.219, f32[128,128]{0,1:T(8,128)S(1)} %get-tuple-element.955, f32[128]{0:T(128)S(1)} %convert_multiply_fusion.2, f32[256,128]{0,1:T(8,128)S(1)} %bitcast.220, ...), kind=kOutput, calls=%fused_computation.75.clone.3 | convolution fusion | flops 328204288 | bytes 6882433 | tf_op jit(solution)/shard_map/while/body/eval_jaxpr/rsi,sci->rci/dot_general | solution.py:114
  373.8 11.1 %bitcast_add_fusion.7 = f32[128,32,128]{0,1,2:T(8,128)} fusion(f32[128,32,128]{0,1,2:T(8,128)} %get-tuple-element.974, f32[256,128]{0,1:T(8,128)S(1)} %bitcast.219, f32[128,128]{0,1:T(8,128)S(1)} %get-tuple-element.955, f32[128]{0:T(128)S(1)} %convert_multiply_fusion.2, f32[256,128]{0,1:T(8,128)S(1)} %bitcast.220, ...), kind=kOutput, calls=%fused_computation.75.clone.3 | convolution fusion | flops 328204288 | bytes 6882433 | tf_op jit(solution)/shard_map/while/body/eval_jaxpr/rsi,sci->rci/dot_general | solution.py:114
  391.2 11.1 %bitcast_add_fusion.7 = f32[128,32,128]{0,1,2:T(8,128)} fusion(f32[128,32,128]{0,1,2:T(8,128)} %get-tuple-element.974, f32[256,128]{0,1:T(8,128)S(1)} %bitcast.219, f32[128,128]{0,1:T(8,128)S(1)} %get-tuple-element.955, f32[128]{0:T(128)S(1)} %convert_multiply_fusion.2, f32[256,128]{0,1:T(8,128)S(1)} %bitcast.220, ...), kind=kOutput, calls=%fused_computation.75.clone.3 | convolution fusion | flops 328204288 | bytes 6882433 | tf_op jit(solution)/shard_map/while/body/eval_jaxpr/rsi,sci->rci/dot_general | solution.py:114
  408.6 11.1 %bitcast_add_fusion.7 = f32[128,32,128]{0,1,2:T(8,128)} fusion(f32[128,32,128]{0,1,2:T(8,128)} %get-tuple-element.974, f32[256,128]{0,1:T(8,128)S(1)} %bitcast.219, f32[128,128]{0,1:T(8,128)S(1)} %get-tuple-element.955, f32[128]{0:T(128)S(1)} %convert_multiply_fusion.2, f32[256,128]{0,1:T(8,128)S(1)} %bitcast.220, ...), kind=kOutput, calls=%fused_computation.75.clone.3 | convolution fusion | flops 328204288 | bytes 6882433 | tf_op jit(solution)/shard_map/while/body/eval_jaxpr/rsi,sci->rci/dot_general | solution.py:114
  425.9 11.1 %bitcast_add_fusion.7 = f32[128,32,128]{0,1,2:T(8,128)} fusion(f32[128,32,128]{0,1,2:T(8,128)} %get-tuple-element.974, f32[256,128]{0,1:T(8,128)S(1)} %bitcast.219, f32[128,128]{0,1:T(8,128)S(1)} %get-tuple-element.955, f32[128]{0:T(128)S(1)} %convert_multiply_fusion.2, f32[256,128]{0,1:T(8,128)S(1)} %bitcast.220, ...), kind=kOutput, calls=%fused_computation.75.clone.3 | convolution fusion | flops 328204288 | bytes 6882433 | tf_op jit(solution)/shard_map/while/body/eval_jaxpr/rsi,sci->rci/dot_general | solution.py:114
  443.3 11.1 %bitcast_add_fusion.7 = f32[128,32,128]{0,1,2:T(8,128)} fusion(f32[128,32,128]{0,1,2:T(8,128)} %get-tuple-element.974, f32[256,128]{0,1:T(8,128)S(1)} %bitcast.219, f32[128,128]{0,1:T(8,128)S(1)} %get-tuple-element.955, f32[128]{0:T(128)S(1)} %convert_multiply_fusion.2, f32[256,128]{0,1:T(8,128)S(1)} %bitcast.220, ...), kind=kOutput, calls=%fused_computation.75.clone.3 | convolution fusion | flops 328204288 | bytes 6882433 | tf_op jit(solution)/shard_map/while/body/eval_jaxpr/rsi,sci->rci/dot_general | solution.py:114
  460.7 11.1 %bitcast_add_fusion.7 = f32[128,32,128]{0,1,2:T(8,128)} fusion(f32[128,32,128]{0,1,2:T(8,128)} %get-tuple-element.974, f32[256,128]{0,1:T(8,128)S(1)} %bitcast.219, f32[128,128]{0,1:T(8,128)S(1)} %get-tuple-element.955, f32[128]{0:T(128)S(1)} %convert_multiply_fusion.2, f32[256,128]{0,1:T(8,128)S(1)} %bitcast.220, ...), kind=kOutput, calls=%fused_computation.75.clone.3 | convolution fusion | flops 328204288 | bytes 6882433 | tf_op jit(solution)/shard_map/while/body/eval_jaxpr/rsi,sci->rci/dot_general | solution.py:114
  478.1 11.1 %bitcast_add_fusion.7 = f32[128,32,128]{0,1,2:T(8,128)} fusion(f32[128,32,128]{0,1,2:T(8,128)} %get-tuple-element.974, f32[256,128]{0,1:T(8,128)S(1)} %bitcast.219, f32[128,128]{0,1:T(8,128)S(1)} %get-tuple-element.955, f32[128]{0:T(128)S(1)} %convert_multiply_fusion.2, f32[256,128]{0,1:T(8,128)S(1)} %bitcast.220, ...), kind=kOutput, calls=%fused_computation.75.clone.3 | convolution fusion | flops 328204288 | bytes 6882433 | tf_op jit(solution)/shard_map/while/body/eval_jaxpr/rsi,sci->rci/dot_general | solution.py:114
  495.4 11.1 %bitcast_add_fusion.7 = f32[128,32,128]{0,1,2:T(8,128)} fusion(f32[128,32,128]{0,1,2:T(8,128)} %get-tuple-element.974, f32[256,128]{0,1:T(8,128)S(1)} %bitcast.219, f32[128,128]{0,1:T(8,128)S(1)} %get-tuple-element.955, f32[128]{0:T(128)S(1)} %convert_multiply_fusion.2, f32[256,128]{0,1:T(8,128)S(1)} %bitcast.220, ...), kind=kOutput, calls=%fused_computation.75.clone.3 | convolution fusion | flops 328204288 | bytes 6882433 | tf_op jit(solution)/shard_map/while/body/eval_jaxpr/rsi,sci->rci/dot_general | solution.py:114
  512.8 11.1 %bitcast_add_fusion.7 = f32[128,32,128]{0,1,2:T(8,128)} fusion(f32[128,32,128]{0,1,2:T(8,128)} %get-tuple-element.974, f32[256,128]{0,1:T(8,128)S(1)} %bitcast.219, f32[128,128]{0,1:T(8,128)S(1)} %get-tuple-element.955, f32[128]{0:T(128)S(1)} %convert_multiply_fusion.2, f32[256,128]{0,1:T(8,128)S(1)} %bitcast.220, ...), kind=kOutput, calls=%fused_computation.75.clone.3 | convolution fusion | flops 328204288 | bytes 6882433 | tf_op jit(solution)/shard_map/while/body/eval_jaxpr/rsi,sci->rci/dot_general | solution.py:114
  530.2 11.1 %bitcast_add_fusion.7 = f32[128,32,128]{0,1,2:T(8,128)} fusion(f32[128,32,128]{0,1,2:T(8,128)} %get-tuple-element.974, f32[256,128]{0,1:T(8,128)S(1)} %bitcast.219, f32[128,128]{0,1:T(8,128)S(1)} %get-tuple-element.955, f32[128]{0:T(128)S(1)} %convert_multiply_fusion.2, f32[256,128]{0,1:T(8,128)S(1)} %bitcast.220, ...), kind=kOutput, calls=%fused_computation.75.clone.3 | convolution fusion | flops 328204288 | bytes 6882433 | tf_op jit(solution)/shard_map/while/body/eval_jaxpr/rsi,sci->rci/dot_general | solution.py:114
  547.5 11.1 %bitcast_add_fusion.7 = f32[128,32,128]{0,1,2:T(8,128)} fusion(f32[128,32,128]{0,1,2:T(8,128)} %get-tuple-element.974, f32[256,128]{0,1:T(8,128)S(1)} %bitcast.219, f32[128,128]{0,1:T(8,128)S(1)} %get-tuple-element.955, f32[128]{0:T(128)S(1)} %convert_multiply_fusion.2, f32[256,128]{0,1:T(8,128)S(1)} %bitcast.220, ...), kind=kOutput, calls=%fused_computation.75.clone.3 | convolution fusion | flops 328204288 | bytes 6882433 | tf_op jit(solution)/shard_map/while/body/eval_jaxpr/rsi,sci->rci/dot_general | solution.py:114
  564.9 11.1 %bitcast_add_fusion.7 = f32[128,32,128]{0,1,2:T(8,128)} fusion(f32[128,32,128]{0,1,2:T(8,128)} %get-tuple-element.974, f32[256,128]{0,1:T(8,128)S(1)} %bitcast.219, f32[128,128]{0,1:T(8,128)S(1)} %get-tuple-element.955, f32[128]{0:T(128)S(1)} %convert_multiply_fusion.2, f32[256,128]{0,1:T(8,128)S(1)} %bitcast.220, ...), kind=kOutput, calls=%fused_computation.75.clone.3 | convolution fusion | flops 328204288 | bytes 6882433 | tf_op jit(solution)/shard_map/while/body/eval_jaxpr/rsi,sci->rci/dot_general | solution.py:114
  582.3 11.1 %bitcast_add_fusion.7 = f32[128,32,128]{0,1,2:T(8,128)} fusion(f32[128,32,128]{0,1,2:T(8,128)} %get-tuple-element.974, f32[256,128]{0,1:T(8,128)S(1)} %bitcast.219, f32[128,128]{0,1:T(8,128)S(1)} %get-tuple-element.955, f32[128]{0:T(128)S(1)} %convert_multiply_fusion.2, f32[256,128]{0,1:T(8,128)S(1)} %bitcast.220, ...), kind=kOutput, calls=%fused_computation.75.clone.3 | convolution fusion | flops 328204288 | bytes 6882433 | tf_op jit(solution)/shard_map/while/body/eval_jaxpr/rsi,sci->rci/dot_general | solution.py:114
  599.7 11.1 %bitcast_add_fusion.7 = f32[128,32,128]{0,1,2:T(8,128)} fusion(f32[128,32,128]{0,1,2:T(8,128)} %get-tuple-element.974, f32[256,128]{0,1:T(8,128)S(1)} %bitcast.219, f32[128,128]{0,1:T(8,128)S(1)} %get-tuple-element.955, f32[128]{0:T(128)S(1)} %convert_multiply_fusion.2, f32[256,128]{0,1:T(8,128)S(1)} %bitcast.220, ...), kind=kOutput, calls=%fused_computation.75.clone.3 | convolution fusion | flops 328204288 | bytes 6882433 | tf_op jit(solution)/shard_map/while/body/eval_jaxpr/rsi,sci->rci/dot_general | solution.py:114
  617.0 11.1 %bitcast_add_fusion.7 = f32[128,32,128]{0,1,2:T(8,128)} fusion(f32[128,32,128]{0,1,2:T(8,128)} %get-tuple-element.974, f32[256,128]{0,1:T(8,128)S(1)} %bitcast.219, f32[128,128]{0,1:T(8,128)S(1)} %get-tuple-element.955, f32[128]{0:T(128)S(1)} %convert_multiply_fusion.2, f32[256,128]{0,1:T(8,128)S(1)} %bitcast.220, ...), kind=kOutput, calls=%fused_computation.75.clone.3 | convolution fusion | flops 328204288 | bytes 6882433 | tf_op jit(solution)/shard_map/while/body/eval_jaxpr/rsi,sci->rci/dot_general | solution.py:114
  634.4 11.1 %bitcast_add_fusion.7 = f32[128,32,128]{0,1,2:T(8,128)} fusion(f32[128,32,128]{0,1,2:T(8,128)} %get-tuple-element.974, f32[256,128]{0,1:T(8,128)S(1)} %bitcast.219, f32[128,128]{0,1:T(8,128)S(1)} %get-tuple-element.955, f32[128]{0:T(128)S(1)} %convert_multiply_fusion.2, f32[256,128]{0,1:T(8,128)S(1)} %bitcast.220, ...), kind=kOutput, calls=%fused_computation.75.clone.3 | convolution fusion | flops 328204288 | bytes 6882433 | tf_op jit(solution)/shard_map/while/body/eval_jaxpr/rsi,sci->rci/dot_general | solution.py:114
  651.8 11.1 %bitcast_add_fusion.7 = f32[128,32,128]{0,1,2:T(8,128)} fusion(f32[128,32,128]{0,1,2:T(8,128)} %get-tuple-element.974, f32[256,128]{0,1:T(8,128)S(1)} %bitcast.219, f32[128,128]{0,1:T(8,128)S(1)} %get-tuple-element.955, f32[128]{0:T(128)S(1)} %convert_multiply_fusion.2, f32[256,128]{0,1:T(8,128)S(1)} %bitcast.220, ...), kind=kOutput, calls=%fused_computation.75.clone.3 | convolution fusion | flops 328204288 | bytes 6882433 | tf_op jit(solution)/shard_map/while/body/eval_jaxpr/rsi,sci->rci/dot_general | solution.py:114
  669.1 11.1 %bitcast_add_fusion.7 = f32[128,32,128]{0,1,2:T(8,128)} fusion(f32[128,32,128]{0,1,2:T(8,128)} %get-tuple-element.974, f32[256,128]{0,1:T(8,128)S(1)} %bitcast.219, f32[128,128]{0,1:T(8,128)S(1)} %get-tuple-element.955, f32[128]{0:T(128)S(1)} %convert_multiply_fusion.2, f32[256,128]{0,1:T(8,128)S(1)} %bitcast.220, ...), kind=kOutput, calls=%fused_computation.75.clone.3 | convolution fusion | flops 328204288 | bytes 6882433 | tf_op jit(solution)/shard_map/while/body/eval_jaxpr/rsi,sci->rci/dot_general | solution.py:114
  686.5 11.1 %bitcast_add_fusion.7 = f32[128,32,128]{0,1,2:T(8,128)} fusion(f32[128,32,128]{0,1,2:T(8,128)} %get-tuple-element.974, f32[256,128]{0,1:T(8,128)S(1)} %bitcast.219, f32[128,128]{0,1:T(8,128)S(1)} %get-tuple-element.955, f32[128]{0:T(128)S(1)} %convert_multiply_fusion.2, f32[256,128]{0,1:T(8,128)S(1)} %bitcast.220, ...), kind=kOutput, calls=%fused_computation.75.clone.3 | convolution fusion | flops 328204288 | bytes 6882433 | tf_op jit(solution)/shard_map/while/body/eval_jaxpr/rsi,sci->rci/dot_general | solution.py:114
  703.9 11.1 %bitcast_add_fusion.7 = f32[128,32,128]{0,1,2:T(8,128)} fusion(f32[128,32,128]{0,1,2:T(8,128)} %get-tuple-element.974, f32[256,128]{0,1:T(8,128)S(1)} %bitcast.219, f32[128,128]{0,1:T(8,128)S(1)} %get-tuple-element.955, f32[128]{0:T(128)S(1)} %convert_multiply_fusion.2, f32[256,128]{0,1:T(8,128)S(1)} %bitcast.220, ...), kind=kOutput, calls=%fused_computation.75.clone.3 | convolution fusion | flops 328204288 | bytes 6882433 | tf_op jit(solution)/shard_map/while/body/eval_jaxpr/rsi,sci->rci/dot_general | solution.py:114
  721.3 11.1 %bitcast_add_fusion.7 = f32[128,32,128]{0,1,2:T(8,128)} fusion(f32[128,32,128]{0,1,2:T(8,128)} %get-tuple-element.974, f32[256,128]{0,1:T(8,128)S(1)} %bitcast.219, f32[128,128]{0,1:T(8,128)S(1)} %get-tuple-element.955, f32[128]{0:T(128)S(1)} %convert_multiply_fusion.2, f32[256,128]{0,1:T(8,128)S(1)} %bitcast.220, ...), kind=kOutput, calls=%fused_computation.75.clone.3 | convolution fusion | flops 328204288 | bytes 6882433 | tf_op jit(solution)/shard_map/while/body/eval_jaxpr/rsi,sci->rci/dot_general | solution.py:114
  (593 shorter events, 260.4 us)
Async XLA Ops:
  6.5 228.5 %copy-start = (s32[16,16]{1,0:T(8,128)S(1)}, s32[16,16]{1,0:T(8,128)}, u32[]{:S(2)}) copy-start(s32[16,16]{1,0:T(8,128)} %param.25) | copy-start | bytes 3076
  6.5 260.5 %all-reduce.4.cloned.1.call-start = ((), (), s32[]{:S(2)}) async-start(), calls=%async_computation.1 | async-start | bytes 4194304 | tf_op jit(solution)/shard_map/psum | solution.py:145
  9.1 4.2 copy-start.1
  15.8 58.9 %copy-start.4 = (bf16[3,64,128]{2,1,0:T(8,128)(2,1)S(1)}, bf16[3,64,128]{2,1,0:T(8,128)(2,1)}, u32[]{:S(2)}) copy-start(bf16[3,64,128]{2,1,0:T(8,128)(2,1)} %param.20) | copy-start | bytes 147460
  15.8 64.3 %copy-start.7 = (s32[16,128]{1,0:T(8,128)S(1)}, s32[16,128]{1,0:T(8,128)}, u32[]{:S(2)}) copy-start(s32[16,128]{1,0:T(8,128)} %param.24) | copy-start | bytes 24580
  68.7 16.8 %collective-permute-start.4 = (bf16[64,32,47]{0,1,2:T(8,128)(2,1)}, bf16[64,32,47]{0,1,2:T(8,128)(2,1)}, u32[]{:S(2)}, u32[]{:S(2)}) collective-permute-start(bf16[64,32,47]{0,1,2:T(8,128)(2,1)} %get-tuple-element.781), channel_id=1, source_target_pairs={{0,4},{4,8},{8,12},{1,5},{5,9},{9,13},{2,6},{6,10},{10,14},{3,7},{... | collective-permute-start | bytes 577544 | tf_op jit(solution)/shard_map/ppermute | solution.py:23
  71.9 13.6 %collective-permute-start.5 = (bf16[64,32,47]{0,1,2:T(8,128)(2,1)}, bf16[64,32,47]{0,1,2:T(8,128)(2,1)}, u32[]{:S(2)}, u32[]{:S(2)}) collective-permute-start(bf16[64,32,47]{0,1,2:T(8,128)(2,1)} %get-tuple-element.782), channel_id=1, source_target_pairs={{4,0},{8,4},{12,8},{5,1},{9,5},{13,9},{6,2},{10,6},{14,10},{7,3},{... | collective-permute-start | bytes 577544 | tf_op jit(solution)/shard_map/ppermute | solution.py:25
  74.8 5.8 collective-permute-start.6
  77.3 6.4 collective-permute-start.7
  188.9 109.2 %all-gather.2.cloned.1.call-start = ((), (), s32[]{:S(2)}) async-start(), calls=%async_computation | async-start | bytes 4030464 | tf_op jit(solution)/shard_map/all_gather | solution.py:99
  190.7 44.4 %collective-permute-start = (bf16[128,32,18]{0,1,2:T(8,128)(2,1)}, bf16[128,32,18]{0,1,2:T(8,128)(2,1)}, u32[]{:S(2)}, u32[]{:S(2)}) collective-permute-start(bf16[128,32,18]{0,1,2:T(8,128)(2,1)} %get-tuple-element.783), channel_id=1, source_target_pairs={{0,4},{4,8},{8,12},{1,5},{5,9},{9,13},{2,6},{6,10},{10,14},{3,7},{... | collective-permute-start | bytes 442376 | tf_op jit(solution)/shard_map/ppermute | solution.py:23
  194.1 41.0 %collective-permute-start.1 = (bf16[128,32,18]{0,1,2:T(8,128)(2,1)}, bf16[128,32,18]{0,1,2:T(8,128)(2,1)}, u32[]{:S(2)}, u32[]{:S(2)}) collective-permute-start(bf16[128,32,18]{0,1,2:T(8,128)(2,1)} %get-tuple-element.784), channel_id=1, source_target_pairs={{4,0},{8,4},{12,8},{5,1},{9,5},{13,9},{6,2},{10,6},{14,10},{7,3},{... | collective-permute-start | bytes 442376 | tf_op jit(solution)/shard_map/ppermute | solution.py:25
  197.8 13.7 %copy-start.3 = (bf16[3,256,128]{1,0,2:T(4,128)(2,1)}, bf16[3,256,128]{1,0,2:T(4,128)(2,1)S(1)}, u32[]{:S(2)}) copy-start(bf16[3,256,128]{1,0,2:T(4,128)(2,1)S(1)} %copy.55) | copy-start | bytes 589828
  198.6 67.2 %collective-permute-start.2 = (bf16[3,256,18]{1,0,2:T(4,128)(2,1)}, bf16[3,256,18]{1,0,2:T(4,128)(2,1)}, u32[]{:S(2)}, u32[]{:S(2)}) collective-permute-start(bf16[3,256,18]{1,0,2:T(4,128)(2,1)} %get-tuple-element.785), channel_id=1, source_target_pairs={{0,4},{4,8},{8,12},{1,5},{5,9},{9,13},{2,6},{6,10},{10,14},{3,7},{... | collective-permute-start | bytes 82952 | tf_op jit(solution)/shard_map/ppermute | solution.py:23
  201.3 64.5 %collective-permute-start.3 = (bf16[3,256,18]{1,0,2:T(4,128)(2,1)S(1)}, bf16[3,256,18]{1,0,2:T(4,128)(2,1)}, u32[]{:S(2)}, u32[]{:S(2)}) collective-permute-start(bf16[3,256,18]{1,0,2:T(4,128)(2,1)S(1)} %get-tuple-element.786), channel_id=1, source_target_pairs={{4,0},{8,4},{12,8},{5,1},{9,5},{13,9},{6,2},{10,6},{14,10},{7,3},{... | collective-permute-start | bytes 82952 | tf_op jit(solution)/shard_map/ppermute | solution.py:25
  209.2 14.6 %copy-start.5 = (bf16[3,64,16]{1,2,0:T(8,128)(2,1)S(1)}, bf16[3,64,16]{1,2,0:T(8,128)(2,1)}, u32[]{:S(2)}) copy-start(bf16[3,64,16]{1,2,0:T(8,128)(2,1)} %param.21) | copy-start | bytes 18436
  267.0 31.1 %copy-start.6 = (s32[128]{0:T(128)S(1)}, s32[128]{0:T(128)}, u32[]{:S(2)}) copy-start(s32[128]{0:T(128)} %param.23) | copy-start | bytes 1540
  302.7 1.7 copy-start.2
  320.0 1.7 copy-start.2
  337.4 1.7 copy-start.2
  354.8 1.7 copy-start.2
  372.1 1.7 copy-start.2
  389.5 1.7 copy-start.2
  406.9 1.7 copy-start.2
  424.3 1.7 copy-start.2
  441.6 1.7 copy-start.2
  459.0 1.7 copy-start.2
  476.4 1.7 copy-start.2
  493.7 1.7 copy-start.2
  511.1 1.7 copy-start.2
  528.5 1.7 copy-start.2
  545.8 1.7 copy-start.2
  563.2 1.7 copy-start.2
  580.6 1.7 copy-start.2
  598.0 1.7 copy-start.2
  615.3 1.7 copy-start.2
  632.7 1.7 copy-start.2
  650.1 1.7 copy-start.2
  667.4 1.7 copy-start.2
  684.8 1.7 copy-start.2
  702.2 1.7 copy-start.2
  719.6 1.7 copy-start.2
Sparse Core Ops, SparseCore 0:
  189.1 64.8 all-reduce.3
  255.6 42.4 all-gather.1
where the time goes:
time: 751 us; the launch traced here: 744 us
  matrix products  347 us (46%)
  local copies, waits for them, and re-layouts  152 us (20%)
  other arithmetic  91.7 us (12%)
  blocking collectives  83.8 us (11%)
  waiting for transfers between devices  29.1 us (4%)
  starting transfers between devices  23.1 us (3%)
  between operations  13.7 us (2%)
    dot_general x25, matrix products, near_step(): jnp.einsum('rsi,sci->rci', near_tile, sources, preferred_element_type=jnp...  277 us
    gather x25, local copies, waits for them, and re-layouts, near_step(): sources = jnp.take(border_charges, local_ids, axis=2)  61 us
    dot_general x16, matrix products, far_step(): jnp.einsum('abi,bci->aci', far_tile, sources, preferred_element_type=jnp....  59.8 us
    psum x1, blocking collectives, per_device(): moments0 = lax.psum(partial_moments, 'near').astype(jnp.bfloat16)  51.9 us
    dot_general x25, other arithmetic, near_step(): jnp.einsum('rsi,sci->rci', near_tile, sources, preferred_element_type=jnp...  40.8 us
    gather x16, local copies, waits for them, and re-layouts, far_step(): sources = jnp.take(source_moments, source_ids, axis=2)  30 us
    all_gather x1, waiting for transfers between devices, per_device(): border_charges = lax.all_gather(thin_charges, 'near', axis=0, tiled=True)  25.6 us
    gather x25, local copies, waits for them, and re-layouts, near_step(): jnp.take(border_points, local_ids, axis=2)  20.9 us
  transfers between devices with their start and end apart: 10, of which 3 were waited for; matrix products, arithmetic and copies ran while one was open for 6% of the time, Pallas kernels for 0%

commit v1 on v0

v1 whole, which is shorter than its diff:
```python
import functools

import jax
import jax.numpy as jnp
import numpy as np
from jax import lax
from jax.experimental import pallas as pl
from jax.experimental.pallas import tpu as pltpu
from jax.sharding import PartitionSpec as P

STRIP = 8
GROUP = 4
FEATURES = 16

softening = 0.25
spacing = 16.0
near_power = 16.0
far_power = 256.0


def padded(cells, axis, width):
    count = lax.axis_size(axis)
    ends = count - 1
    head = cells[:width]
    tail = cells[cells.shape[0] - width :]
    return jnp.concatenate(
        [
            lax.ppermute(tail, axis, [(i, i + 1) for i in range(ends)]),
            cells,
            lax.ppermute(head, axis, [(i + 1, i) for i in range(ends)]),
        ],
        axis=0,
    )


def rotated(cells, axis, step):
    count = lax.axis_size(axis)
    return lax.ppermute(cells, axis, [((i + step) % count, i) for i in range(count)])


def paired(cells, axis_index, dim):
    other = rotated(cells, "rhs", 1)
    first = axis_index == 0
    return jnp.concatenate(
        [jnp.where(first, cells, other), jnp.where(first, other, cells)], axis=dim
    )


def pieces(value):
    top = value.astype(jnp.bfloat16).astype(jnp.float32)
    middle = (value - top).astype(jnp.bfloat16).astype(jnp.float32)
    return [top, middle, value - top - middle]


def offset_tables(width):
    factor = np.zeros((26, FEATURES), np.float32)
    added = np.zeros((26, FEATURES), np.float32)
    factor[:, :9] = 1.0
    factor[:, 14] = 1.0
    for o in range(25):
        shift_x = -spacing * (o % 5 - 2)
        shift_y = -spacing * (o // 5 - 2)
        factor[o, 11] = -2.0 * shift_x
        factor[o, 12] = -2.0 * shift_y
        added[o, 9] = 2.0 * shift_x * near_power
        added[o, 10] = 2.0 * shift_y * near_power
        added[o, 13] = (shift_x * shift_x + shift_y * shift_y) * near_power
    added[25, 13] = np.inf
    spread = lambda t: jnp.asarray(np.repeat(t[:, :, None], width, axis=2), jnp.bfloat16)
    return spread(factor), spread(added)


def row_features(cells):
    x, y, z = cells[0:1], cells[1:2], cells[2:3]
    one = jnp.ones_like(x)
    norm = pieces(x * x + y * y + z * z)
    parts = [x, y, z] + norm + [one] * 3 + [x, y] + [one] * 4 + [jnp.zeros_like(x)]
    return jnp.concatenate(parts, axis=0)


def column_features(cells, power, shifted):
    x, y, z = cells[0:1], cells[1:2], cells[2:3]
    one = jnp.ones_like(x)
    zero = jnp.zeros_like(x)
    norm = pieces(x * x + y * y + z * z)
    parts = (
        [-2.0 * x, -2.0 * y, -2.0 * z]
        + [one] * 3
        + norm
        + [zero, zero]
        + ([x, y] if shifted else [zero, zero])
        + [zero, softening * one, zero]
    )
    return jnp.concatenate(parts, axis=0) * power


def near_kernel(
    slots,
    shares,
    codes_ref,
    groups_ref,
    own_ref,
    border_ref,
    factor_ref,
    added_ref,
    *refs,
):
    charge_refs = refs[:shares]
    out_ref, base_ref, rows_ref, tiles_ref, leaf_at, code_at = refs[shares:]
    leaves = out_ref.shape[0]
    width = border_ref.shape[2]

    def base_step(j, _):
        base_ref[j] = column_features(border_ref[j], near_power, True).astype(jnp.bfloat16)
        return 0

    lax.fori_loop(0, border_ref.shape[0], base_step, 0, unroll=2)

    def row_step(i, at):
        rows_ref[i] = jnp.transpose(row_features(own_ref[i])).astype(jnp.bfloat16)
        out_ref[i] = jnp.zeros(out_ref.shape[1:], jnp.float32)

        def list_step(g, at):
            leaf_at[at] = i
            code_at[at] = i * slots + g * GROUP
            return at + 1

        return lax.fori_loop(0, groups_ref[i], list_step, at)

    total = lax.fori_loop(0, leaves, row_step, 0)
    for spare in range(3):
        leaf_at[total + spare] = 0
        code_at[total + spare] = leaves * slots

    def tile_stage(at, slot):
        row = rows_ref[leaf_at[at]]
        start = code_at[at]
        for u in range(GROUP):
            code = codes_ref[start + u]
            column = base_ref[code // 32] * factor_ref[code % 32] + added_ref[code % 32]
            square = jnp.dot(row, column, preferred_element_type=jnp.float32)
            tiles_ref[slot, :, u * width : (u + 1) * width] = lax.rsqrt(square).astype(jnp.bfloat16)

    def sum_stage(at, slot):
        start = code_at[at]
        i = leaf_at[at]
        sources = []
        for u in range(GROUP):
            j = codes_ref[start + u] // 32
            sources += [ref[j] for ref in charge_refs]
        out_ref[i] += lax.dot_general(
            tiles_ref[slot],
            jnp.concatenate(sources, axis=1),
            (((1,), (1,)), ((), ())),
            preferred_element_type=jnp.float32,
        )

    tile_stage(0, 0)

    def pair_step(t, _):
        at = 2 * t
        tile_stage(at + 1, 1)
        sum_stage(at, 0)
        tile_stage(at + 2, 0)
        sum_stage(at + 1, 1)
        return 0

    lax.fori_loop(0, (total + 1) // 2, pair_step, 0)


def far_kernel(
    leaf_slots,
    parent_slots,
    leaf_reach,
    leaf_ids_ref,
    parent_ids_ref,
    own_start_ref,
    leaf_skeleton_ref,
    leaf_moments_ref,
    parent_skeleton_ref,
    parent_moments_ref,
    transfer_ref,
    basis_ref,
    near_ref,
    out_ref,
    leaf_cols_ref,
    parent_cols_ref,
):
    parents = out_ref.shape[0] // STRIP

    def fill(skeleton_ref, cols_ref):
        def step(j, _):
            columns = column_features(skeleton_ref[j], far_power, False)
            cols_ref[j] = jnp.transpose(columns).astype(jnp.bfloat16)
            return 0

        lax.fori_loop(0, skeleton_ref.shape[0], step, 0, unroll=2)

    fill(leaf_skeleton_ref, leaf_cols_ref)
    fill(parent_skeleton_ref, parent_cols_ref)

    def coupled(cells, slots, start, ids_ref, cols_ref, moments_ref):
        row = jnp.transpose(row_features(cells)).astype(jnp.bfloat16)
        ids = [ids_ref[start + u] for u in range(slots)]
        column = jnp.concatenate([cols_ref[j] for j in ids], axis=0)
        square = lax.dot_general(
            row, column, (((1,), (1,)), ((), ())), preferred_element_type=jnp.float32
        )
        return jnp.dot(
            lax.rsqrt(square).astype(jnp.bfloat16),
            jnp.concatenate([moments_ref[j] for j in ids], axis=0),
            preferred_element_type=jnp.float32,
        )

    def parent_step(p, _):
        parent_field = coupled(
            parent_skeleton_ref[own_start_ref[0] + p],
            parent_slots,
            p * parent_slots,
            parent_ids_ref,
            parent_cols_ref,
            parent_moments_ref,
        ).astype(jnp.bfloat16)

        def leaf_step(child, _):
            i = p * STRIP + child
            field = coupled(
                leaf_skeleton_ref[leaf_reach + i],
                leaf_slots,
                i * leaf_slots,
                leaf_ids_ref,
                leaf_cols_ref,
                leaf_moments_ref,
            )
            leaf_field = field + jnp.dot(
                transfer_ref[i], parent_field, preferred_element_type=jnp.float32
            )
            far = jnp.dot(
                basis_ref[i], leaf_field.astype(jnp.bfloat16), preferred_element_type=jnp.float32
            )
            out_ref[i] = (near_ref[i] + far).astype(out_ref.dtype)
            return 0

        lax.fori_loop(0, STRIP, leaf_step, 0, unroll=4)
        return 0

    lax.fori_loop(0, parents, parent_step, 0)


def in_smem(count):
    return [pl.BlockSpec(memory_space=pltpu.SMEM)] * count


def in_vmem(count):
    return [pl.BlockSpec(memory_space=pltpu.VMEM)] * count


def per_device(
    points,
    charges,
    basis,
    transfer,
    leaf_skeleton,
    parent_skeleton,
    near_list,
    near_count,
    leaf_far,
    parent_far,
):
    rows_here, columns, leaf_count = charges.shape
    rank_size = basis.shape[1]
    near_index = lax.axis_index("near")
    leaf_index = lax.axis_index("leaf")
    rhs_index = lax.axis_index("rhs")
    rhs_parts = lax.axis_size("rhs")
    near_reach = 2 * STRIP + 2
    far_reach = 6 * STRIP - 1
    own = leaf_count // rhs_parts
    own_parents = own // STRIP
    own_start = rhs_index * own
    first_leaf = leaf_index * leaf_count + own_start
    all_columns = columns * rhs_parts

    def mine(array, dim, width=own, start=own_start):
        return lax.dynamic_slice_in_dim(array, start, width, dim)

    leaf_parts = lax.axis_size("leaf")
    near_parts = lax.axis_size("near")
    window = own + 2 * near_reach

    wide = paired(jnp.transpose(charges, (2, 1, 0)), rhs_index, 1)
    wide = mine(padded(wide, "leaf", near_reach), 0, window)
    shares = [wide] + [rotated(wide, "near", k) for k in range(1, near_parts)]

    point_cells = jnp.transpose(points, (2, 0, 1))
    border_points = mine(padded(point_cells, "leaf", near_reach), 0, window)
    twice = jnp.concatenate([border_points, border_points], axis=2).astype(jnp.float32)
    border_points = mine(twice, 2, point_cells.shape[2], near_index * rows_here)
    own_points = border_points[near_reach : near_reach + own, :, :rows_here]

    listing = mine(near_list, 1)
    counts = mine(near_count, 0)
    row_ids = first_leaf + jnp.arange(own, dtype=jnp.int32)
    live = jnp.arange(near_list.shape[0], dtype=jnp.int32)[:, None] < counts[None, :]
    offset = (
        (listing % STRIP - row_ids[None, :] % STRIP + 2)
        + 5 * (listing // STRIP - row_ids[None, :] // STRIP + 2)
    )
    code = jnp.where(live, (listing - (first_leaf - near_reach)) * 32 + offset, 25)
    slots = -(-near_list.shape[0] // GROUP) * GROUP
    code = jnp.pad(
        jnp.transpose(code), ((0, 1), (0, slots - near_list.shape[0])), constant_values=25
    ).reshape(-1)
    groups = (counts + (GROUP - 1)) // GROUP
    factor, added = offset_tables(border_points.shape[2])

    basis_cells = jnp.transpose(mine(basis, 2), (2, 0, 1))
    own_charges = lax.slice_in_dim(wide, near_reach, near_reach + own, axis=0)
    partial = jnp.einsum(
        "isa,ics->iac", basis_cells, own_charges, preferred_element_type=jnp.float32
    )
    sent = partial.astype(jnp.bfloat16)
    for k in range(1, near_parts):
        partial = partial + rotated(sent, "near", k).astype(jnp.float32)
    moments0 = partial.astype(jnp.bfloat16)
    transfer_cells = jnp.transpose(mine(transfer, 2), (2, 0, 1))
    moments1 = jnp.einsum(
        "pkb,pkc->pbc",
        transfer_cells.reshape(own_parents, STRIP * rank_size, rank_size),
        moments0.reshape(own_parents, STRIP * rank_size, all_columns),
        preferred_element_type=jnp.float32,
    ).astype(jnp.bfloat16)
    chip_parents = paired(moments1, rhs_index, 0)
    turn = lambda cells: jnp.concatenate(
        [cells] + [rotated(cells, "leaf", k) for k in range(1, leaf_parts)], axis=0
    )
    every_moments = turn(chip_parents)
    chip_moments = paired(moments0, rhs_index, 0)
    border_moments = mine(padded(chip_moments, "leaf", far_reach), 0, own + 2 * far_reach)

    near_part = pl.pallas_call(
        functools.partial(near_kernel, slots, near_parts),
        out_shape=jax.ShapeDtypeStruct((own, rows_here, all_columns), jnp.float32),
        in_specs=in_smem(2) + in_vmem(4 + near_parts),
        out_specs=pl.BlockSpec(memory_space=pltpu.VMEM),
        scratch_shapes=[
            pltpu.VMEM((window, FEATURES, border_points.shape[2]), jnp.bfloat16),
            pltpu.VMEM((own, rows_here, FEATURES), jnp.bfloat16),
            pltpu.VMEM((2, rows_here, GROUP * border_points.shape[2]), jnp.bfloat16),
            pltpu.SMEM((own * (slots // GROUP) + 3,), jnp.int32),
            pltpu.SMEM((own * (slots // GROUP) + 3,), jnp.int32),
        ],
        compiler_params=pltpu.CompilerParams(vmem_limit_bytes=48 * 2**20),
        cost_estimate=pl.CostEstimate(
            flops=60 * 10**9, bytes_accessed=16 * 10**6, transcendentals=0
        ),
        name="near_field",
    )(code, groups, own_points, border_points, factor, added, *shares)

    skeleton_cells = jnp.transpose(leaf_skeleton, (2, 0, 1))
    border_skeleton = mine(padded(skeleton_cells, "leaf", far_reach), 0, own + 2 * far_reach)
    parent_cells = jnp.transpose(parent_skeleton, (2, 0, 1))
    every_skeleton = turn(parent_cells)
    parent_start = rhs_index * own_parents
    leaf_ids = jnp.transpose(mine(leaf_far, 1) - (first_leaf - far_reach)).reshape(-1)
    chip_count = parent_far.shape[1]
    parent_ids = jnp.transpose(mine(parent_far, 1, own_parents, parent_start)).reshape(-1)
    parent_ids = (parent_ids + (leaf_parts - leaf_index) * chip_count) % (leaf_parts * chip_count)

    result = pl.pallas_call(
        functools.partial(far_kernel, leaf_far.shape[0], parent_far.shape[0], far_reach),
        out_shape=jax.ShapeDtypeStruct((own, rows_here, all_columns), jnp.bfloat16),
        in_specs=in_smem(3) + in_vmem(7),
        out_specs=pl.BlockSpec(memory_space=pltpu.VMEM),
        scratch_shapes=[
            pltpu.VMEM((own + 2 * far_reach, rank_size, FEATURES), jnp.bfloat16),
            pltpu.VMEM((leaf_parts * chip_count, rank_size, FEATURES), jnp.bfloat16),
        ],
        compiler_params=pltpu.CompilerParams(vmem_limit_bytes=48 * 2**20),
        name="far_field",
    )(
        leaf_ids,
        parent_ids,
        parent_start.astype(jnp.int32).reshape(1),
        border_skeleton.astype(jnp.float32),
        border_moments,
        every_skeleton.astype(jnp.float32),
        every_moments,
        transfer_cells,
        basis_cells,
        near_part,
    )
    result = jnp.transpose(result, (1, 2, 0))
    kept = mine(result, 1, columns, rhs_index * columns)
    given = mine(result, 1, columns, (1 - rhs_index) * columns)
    taken = rotated(given, "rhs", 1)
    first = rhs_index == 0
    return jnp.concatenate(
        [jnp.where(first, kept, taken), jnp.where(first, taken, kept)], axis=2
    )


def solution(mesh):
    placed = (
        P(None, None, ("groups", "leaf")),
        P("near", "rhs", ("groups", "leaf")),
        P("near", None, ("groups", "leaf")),
        P(None, None, ("groups", "leaf")),
        P(None, None, ("groups", "leaf")),
        P(None, None, ("groups", "leaf")),
        P(None, ("groups", "leaf")),
        P(("groups", "leaf")),
        P(None, ("groups", "leaf")),
        P(None, ("groups", "leaf")),
    )
    return jax.shard_map(
        per_device,
        mesh=mesh,
        in_specs=placed,
        out_specs=P("near", "rhs", ("groups", "leaf")),
        check_vma=False,
    )
```

time: 751 us -> 255 us (0.34)
  matrix products: 347 us -> 2.87 us
  local copies, waits for them, and re-layouts: 152 us -> 32.8 us
  Pallas kernels: 0 us -> 118 us
  blocking collectives: 83.8 us -> 0 us
  other arithmetic: 91.7 us -> 24.4 us
  waiting for transfers between devices: 29.1 us -> 43.1 us
  between operations: 13.7 us -> 0.48 us
  starting transfers between devices: 23.1 us -> 33.3 us
    dot_general x44 -> x2, matrix products: 347 us -> 2.87 us  [the longest x1 2.39 us: per_device(): jnp.einsum('isa,ics->iac', basis_cells, own_charges, preferred_element_ty...]
    gather x82 -> x0, local copies, waits for them, and re-layouts: 130 us -> none  [the longest x25 61 us: near_step(): sources = jnp.take(border_charges, local_ids, axis=2)]
    pallas_call x0 -> x2, Pallas kernels: none -> 118 us  [the longest x1 74.7 us: per_device(): pl.pallas_call(functools.partial(near_kernel, slots, near_parts), out_sha...]
    psum x2 -> x0, blocking collectives: 60.4 us -> none  [the longest x1 51.9 us: per_device(): moments0 = lax.psum(partial_moments, 'near').astype(jnp.bfloat16)]
    dot_general x25 -> x0, other arithmetic: 40.8 us -> none  [near_step(): jnp.einsum('rsi,sci->rci', near_tile, sources, preferred_element_type=jnp...]
    ppermute x8 -> x20, waiting for transfers between devices: 3.44 us -> 43.1 us  [the longest x12 41.1 us: rotated(): lax.ppermute(cells, axis, [((i + step) % count, i) for i in range(count)])]
    all_gather x1 -> x0, waiting for transfers between devices: 25.6 us -> none  [per_device(): border_charges = lax.all_gather(thin_charges, 'near', axis=0, tiled=True)]
    all_gather x2 -> x0, blocking collectives: 23.4 us -> none  [the longest x1 12.2 us: per_device(): lax.all_gather(moments1, 'leaf', axis=2, tiled=True)]
  transfers between devices with their start and end apart: 10 -> 20, of which waited for: 3 -> 6; matrix products, arithmetic and copies ran while one was open for 6% -> 13% of each run, Pallas kernels for 0% -> 0%
where the time goes in v1:
time: 255 us; the launch traced here: 254 us
  Pallas kernels  118 us (46%)
  waiting for transfers between devices  43.1 us (17%)
  starting transfers between devices  33.3 us (13%)
  local copies, waits for them, and re-layouts  32.8 us (13%)
  other arithmetic  24.4 us (10%)
  matrix products  2.87 us (1%)
    pallas_call x1, Pallas kernels, per_device(): pl.pallas_call(functools.partial(near_kernel, slots, near_parts), out_sha...  74.7 us
    pallas_call x1, Pallas kernels, per_device(): pl.pallas_call(functools.partial(far_kernel, leaf_far.shape[0], parent_fa...  42.8 us
    ppermute x12, waiting for transfers between devices, rotated(): lax.ppermute(cells, axis, [((i + step) % count, i) for i in range(count)])  41.1 us
    unnamed x45, local copies, waits for them, and re-layouts  14.5 us
    ppermute x12, starting transfers between devices, rotated(): lax.ppermute(cells, axis, [((i + step) % count, i) for i in range(count)])  12 us
    ppermute x4, starting transfers between devices, padded(): lax.ppermute(head, axis, [(i + 1, i) for i in range(ends)])  10.9 us
    ppermute x4, starting transfers between devices, padded(): lax.ppermute(tail, axis, [(i, i + 1) for i in range(ends)])  10.4 us
    concatenate x4, other arithmetic, padded(): jnp.concatenate([lax.ppermute(tail, axis, [(i, i + 1) for i in range(ends...  9.24 us
  transfers between devices with their start and end apart: 20, of which 6 were waited for; matrix products, arithmetic and copies ran while one was open for 13% of the time, Pallas kernels for 0%

profile of v1, /device:TPU:13, one launch (start us, length us, event | category | flops | bytes accessed | tf_op | source)
XLA Modules:
  0.0 254.5 jit_solution(11032865481851179643)
XLA Ops:
  0.0 2.6 %copy.41 = bf16[128,32,128]{0,1,2:T(8,128)(2,1)S(1)} copy(bf16[128,32,128]{2,1,0:T(8,128)(2,1)} %param.13) | data formatting | bytes 2097152 | tf_op args[1]
  2.7 0.7 collective-permute-start.2
  3.4 1.3 collective-permute-start.11
  4.8 1.1 collective-permute-start.10
  5.9 1.4 collective-permute-start.9
  7.3 1.1 copy.48
  8.5 2.0 constant_dynamic-slice_fusion.1
  11.3 1.7 broadcast_select_fusion.1
  13.0 0.9 copy-done.7
  14.0 0.9 pad_maximum_fusion.1
  14.9 3.0 %collective-permute-start.4 = (bf16[18,64,128]{2,1,0:T(8,128)(2,1)}, bf16[18,64,128]{2,1,0:T(8,128)(2,1)}, u32[]{:S(2)}, u32[]{:S(2)}) collective-permute-start(bf16[18,64,128]{2,1,0:T(8,128)(2,1)} %get-tuple-element.15), channel_id=1, source_target_pairs={{4,0},{8,4},{12,8},{5,1},{9,5},{13,9},{6,2},{10,6},{14,10},{7,3},{... | collective-permute-start | bytes 884744 | tf_op jit(solution)/shard_map/ppermute | solution.py:30
  17.9 2.3 collective-permute-start.3
  20.4 4.5 %copy.58 = bf16[128,64,64]{1,0,2:T(8,128)(2,1)} copy(bf16[128,64,64]{2,1,0:T(8,128)(2,1)} %constant_dynamic-slice_fusion.1) | data formatting | bytes 2097152
  25.0 2.8 %collective-permute-start = (bf16[47,3,64]{0,2,1:T(8,128)(2,1)S(1)}, bf16[47,3,64]{0,2,1:T(8,128)(2,1)S(1)}, u32[]{:S(2)}, u32[]{:S(2)}) collective-permute-start(bf16[47,3,64]{0,2,1:T(8,128)(2,1)S(1)} %get-tuple-element.21), channel_id=1, source_target_pairs={{0,4},{4,8},{8,12},{1,5},{5,9},{9,13},{2,6},{6,10},{10,14},{3,7},{... | collective-permute-start | bytes 54152 | tf_op jit(solution)/shard_map/ppermute | solution.py:28
  27.9 2.5 fusion.4.refs_0_
  30.4 2.4 fusion.29
  32.8 1.2 collective-permute-start.5
  34.0 1.4 constant_dynamic-slice_fusion
  35.8 2.6 %copy.59 = bf16[64,64,64]{1,0,2:T(8,128)(2,1)S(1)} copy(bf16[64,64,64]{2,1,0:T(8,128)(2,1)} %constant_dynamic-slice_fusion) | data formatting | bytes 1048576
  38.4 2.6 %collective-permute-start.1 = (bf16[47,3,64]{0,2,1:T(8,128)(2,1)S(1)}, bf16[47,3,64]{0,2,1:T(8,128)(2,1)S(1)}, u32[]{:S(2)}, u32[]{:S(2)}) collective-permute-start(bf16[47,3,64]{0,2,1:T(8,128)(2,1)S(1)} %get-tuple-element.22), channel_id=1, source_target_pairs={{4,0},{8,4},{12,8},{5,1},{9,5},{13,9},{6,2},{10,6},{14,10},{7,3},{... | collective-permute-start | bytes 54152 | tf_op jit(solution)/shard_map/ppermute | solution.py:30
  41.1 1.9 collective-permute-start.17
  43.0 3.4 %collective-permute-start.16 = (bf16[18,3,256]{2,1,0:T(4,128)(2,1)}, bf16[18,3,256]{2,1,0:T(4,128)(2,1)}, u32[]{:S(2)}, u32[]{:S(2)}) collective-permute-start(bf16[18,3,256]{2,1,0:T(4,128)(2,1)} %get-tuple-element.20), channel_id=1, source_target_pairs={{0,4},{4,8},{8,12},{1,5},{5,9},{9,13},{2,6},{6,10},{10,14},{3,7},{... | collective-permute-start | bytes 82952 | tf_op jit(solution)/shard_map/ppermute | solution.py:28
  46.4 0.8 maximum_convert_fusion.parent_skeleton_ref
  47.2 0.8 dynamic-slice_maximum_fusion
  48.0 1.1 copy.57
  49.1 6.9 %collective-permute-done.5 = bf16[64,64,64]{2,1,0:T(8,128)(2,1)} collective-permute-done((bf16[64,64,64]{2,1,0:T(8,128)(2,1)}, bf16[64,64,64]{2,1,0:T(8,128)(2,1)}, u32[]{:S(2)}, u32[]{:S(2)}) %collective-permute-start.5) | collective-permute-done | bytes 524320 | tf_op jit(solution)/shard_map/ppermute | solution.py:38
  56.1 2.2 add_convert_fusion
  58.8 2.6 %collective-permute-start.12 = (bf16[8,64,64]{2,1,0:T(8,128)(2,1)S(1)}, bf16[8,64,64]{2,1,0:T(8,128)(2,1)S(1)}, u32[]{:S(2)}, u32[]{:S(2)}) collective-permute-start(bf16[8,64,64]{2,1,0:T(8,128)(2,1)S(1)} %convolution_convert_fusion), channel_id=1, source_target_pairs={{1,0},{0,1},{3,2},{2,3},{5,4},{4,5},{7,6},{6,7},{9,8},{8,9},{11,10... | collective-permute-start | bytes 196616 | tf_op jit(solution)/shard_map/ppermute | solution.py:38
  61.4 1.1 fusion.9
  62.5 1.3 collective-permute-start.18
  65.9 0.8 collective-permute-done.6
  67.0 1.9 collective-permute-start.7
  68.9 3.4 %collective-permute-start.8 = (bf16[47,64,64]{2,1,0:T(8,128)(2,1)S(1)}, bf16[47,64,64]{2,1,0:T(8,128)(2,1)S(1)}, u32[]{:S(2)}, u32[]{:S(2)}) collective-permute-start(bf16[47,64,64]{2,1,0:T(8,128)(2,1)S(1)} %slice.44), channel_id=1, source_target_pairs={{4,0},{8,4},{12,8},{5,1},{9,5},{13,9},{6,2},{10,6},{14,10},{7,3},{... | collective-permute-start | bytes 1155080 | tf_op jit(solution)/shard_map/ppermute | solution.py:30
  72.6 11.7 %collective-permute-done.13 = bf16[16,64,64]{2,1,0:T(8,128)(2,1)S(1)} collective-permute-done((bf16[16,64,64]{2,1,0:T(8,128)(2,1)S(1)}, bf16[16,64,64]{2,1,0:T(8,128)(2,1)S(1)}, u32[]{:S(2)}, u32[]{:S(2)}) %collective-permute-start.13) | collective-permute-done | bytes 131104 | tf_op jit(solution)/shard_map/ppermute | solution.py:38
  84.4 20.0 %collective-permute-done.15 = bf16[16,64,64]{2,1,0:T(8,128)(2,1)S(1)} collective-permute-done((bf16[16,64,64]{2,1,0:T(8,128)(2,1)S(1)}, bf16[16,64,64]{2,1,0:T(8,128)(2,1)S(1)}, u32[]{:S(2)}, u32[]{:S(2)}) %collective-permute-start.15) | collective-permute-done | bytes 131104 | tf_op jit(solution)/shard_map/ppermute | solution.py:38
  104.5 2.0 collective-permute-done.8
  106.5 4.9 %fusion.2.leaf_moments_ref = bf16[158,64,64]{2,1,0:T(8,128)(2,1)} fusion(s32[]{:T(128)S(6)} %select_n.127, bf16[47,64,64]{2,1,0:T(8,128)(2,1)S(1)} %collective-permute-done.7, bf16[64,64,64]{2,1,0:T(8,128)(2,1)S(1)} %get-tuple-element.13, bf16[64,64,64]{2,1,0:T(8,128)(2,1)S(1)} %get-tuple-element.14, bf16[47,64,64]{2,1,0:T(8,128)(2,1)S(1)} %collective-permute-done.8), kind=kLoop, calls=%fused_computation.10 | loop fusion | flops 1941504 | bytes 3112964 | tf_op jit(solution)/shard_map/concatenate | solution.py:26
  111.3 74.7 %near_field.1.near_ref = f32[64,128,64]{2,1,0:T(8,128)} custom-call(s32[1820]{0:T(1024)S(1)} %reshape.79.codes_ref, s32[64]{0:T(128)S(1)} %get-tuple-element.5.groups_ref, f32[64,3,128]{2,1,0:T(4,128)S(1)} %slice.47.own_ref, f32[100,3,256]{2,1,0:T(4,128)S(1)} %fusion.11.border_ref, bf16[26,16,256]{2,1,0:T(8,128)(2,1)S(1)} %copy-done.5, ...), custom_call_target="tpu_custom_call" | custom-call | flops 60000002048 | bytes 16000000 | tf_op jit(solution)/shard_map/near_field/pallas_call | solution.py:341
  186.1 42.8 %far_field.1 = bf16[64,128,64]{2,1,0:T(8,128)(2,1)S(1)} custom-call(s32[1024]{0:T(1024)S(1)} %reshape.75.leaf_ids_ref, s32[128]{0:T(128)S(1)} %and_select_fusion.3.parent_ids_ref, s32[1]{0:T(128)} %bitcast.2.own_start_ref, f32[158,3,64]{2,1,0:T(4,128)S(1)} %convert_element_type.21.leaf_skeleton_ref, bf16[158,64,64]{2,1,0:T(8,128)(2,1)} %fusion.2.leaf_moments_ref, ...), custom_call_target="tpu_custom_call" | custom-call | tf_op jit(solution)/shard_map/far_field/pallas_call | solution.py:370
  228.9 1.3 copy-done.1
  230.2 2.1 dynamic-slice_bitcast_fusion
  232.4 2.2 copy.49
  235.0 1.6 collective-permute-done.19
  236.6 1.9 copy.50
  238.4 5.9 %bitcast_select_fusion.1 = (bf16[128,32,64]{1,0,2:T(8,128)(2,1)}, bf16[128,32,64]{1,0,2:T(8,128)(2,1)}) fusion(bf16[128,32,64]{1,0,2:T(8,128)(2,1)} %copy.50, pred[]{:T(512)S(6)} %eq.7, bf16[64,128,64]{2,1,0:T(8,128)(2,1)} %copy-done.1, s32[]{:T(128)S(6)} %select_n.145), kind=kLoop, calls=%fused_computation.12 | loop fusion | flops 524288 | bytes 2097157 | tf_op jit(solution)/shard_map/jit(_where)/select_n | solution.py:399
  244.3 3.3 %copy.52 = bf16[128,32,64]{2,1,0:T(8,128)(2,1)S(1)} copy(bf16[128,32,64]{1,0,2:T(8,128)(2,1)} %get-tuple-element.11) | data formatting | bytes 1048576 | tf_op jit(solution)/shard_map/jit(_where)/select_n | solution.py:399
  247.6 4.1 %copy.53 = bf16[128,32,64]{2,1,0:T(8,128)(2,1)} copy(bf16[128,32,64]{1,0,2:T(8,128)(2,1)} %get-tuple-element.12) | data formatting | bytes 1048576 | tf_op jit(solution)/shard_map/jit(_where)/select_n | solution.py:399
  251.7 2.8 %pad_maximum_fusion = bf16[128,32,128]{2,1,0:T(8,128)(2,1)} fusion(bf16[128,32,64]{2,1,0:T(8,128)(2,1)} %copy.53, bf16[128,32,64]{2,1,0:T(8,128)(2,1)S(1)} %copy.52), kind=kLoop, calls=%fused_computation.21 | loop fusion | flops 2097152 | bytes 2097152 | tf_op jit(solution)/shard_map/concatenate | solution.py:398
  (82 shorter events, 5.3 us)
Async XLA Ops:
  0.0 8.5 %copy-start = (bf16[128,64,128]{2,1,0:T(8,128)(2,1)S(1)}, bf16[128,64,128]{2,1,0:T(8,128)(2,1)}, u32[]{:S(2)}) copy-start(bf16[128,64,128]{2,1,0:T(8,128)(2,1)} %param.14) | copy-start | bytes 6291460
  0.0 3.4 %copy-start.14 = (bf16[3,64,16]{1,2,0:T(8,128)(2,1)S(1)}, bf16[3,64,16]{1,2,0:T(8,128)(2,1)}, u32[]{:S(2)}) copy-start(bf16[3,64,16]{1,2,0:T(8,128)(2,1)} %param.17) | copy-start | bytes 18436
  0.0 8.4 %copy-start.17 = (s32[128]{0:T(128)S(1)}, s32[128]{0:T(128)}, u32[]{:S(2)}) copy-start(s32[128]{0:T(128)} %param.19) | copy-start | bytes 1540
  2.7 7.9 %copy-start.8 = (bf16[128,32,128]{0,1,2:T(8,128)(2,1)}, bf16[128,32,128]{0,1,2:T(8,128)(2,1)S(1)}, u32[]{:S(2)}) copy-start(bf16[128,32,128]{0,1,2:T(8,128)(2,1)S(1)} %copy.41) | copy-start | bytes 3145732
  2.7 8.7 %collective-permute-start.2 = (bf16[128,32,128]{2,1,0:T(8,128)(2,1)S(1)}, bf16[128,32,128]{2,1,0:T(8,128)(2,1)}, u32[]{:S(2)}, u32[]{:S(2)}) collective-permute-start(bf16[128,32,128]{2,1,0:T(8,128)(2,1)S(1)} %bitcast.35), channel_id=1, source_target_pairs={{1,0},{0,1},{3,2},{2,3},{5,4},{4,5},{7,6},{6,7},{9,8},{8,9},{11,10... | collective-permute-start | bytes 3145736 | tf_op jit(solution)/shard_map/ppermute | solution.py:38
  3.4 35.0 %collective-permute-start.11 = (bf16[16,3,64]{2,1,0:T(4,128)(2,1)S(1)}, bf16[16,3,64]{2,1,0:T(4,128)(2,1)}, u32[]{:S(2)}, u32[]{:S(2)}) collective-permute-start(bf16[16,3,64]{2,1,0:T(4,128)(2,1)S(1)} %bitcast.40), channel_id=1, source_target_pairs={{12,0},{0,4},{4,8},{8,12},{13,1},{1,5},{5,9},{9,13},{14,2},{2,6},{... | collective-permute-start | bytes 18440 | tf_op jit(solution)/shard_map/ppermute | solution.py:38
  4.8 36.3 %collective-permute-start.10 = (bf16[16,3,64]{2,1,0:T(4,128)(2,1)S(1)}, bf16[16,3,64]{2,1,0:T(4,128)(2,1)}, u32[]{:S(2)}, u32[]{:S(2)}) collective-permute-start(bf16[16,3,64]{2,1,0:T(4,128)(2,1)S(1)} %bitcast.41), channel_id=1, source_target_pairs={{8,0},{12,4},{0,8},{4,12},{9,1},{13,5},{1,9},{5,13},{10,2},{14,6},... | collective-permute-start | bytes 18440 | tf_op jit(solution)/shard_map/ppermute | solution.py:38
  5.9 37.1 %collective-permute-start.9 = (bf16[16,3,64]{2,1,0:T(4,128)(2,1)S(1)}, bf16[16,3,64]{2,1,0:T(4,128)(2,1)}, u32[]{:S(2)}, u32[]{:S(2)}) collective-permute-start(bf16[16,3,64]{2,1,0:T(4,128)(2,1)S(1)} %bitcast.42), channel_id=1, source_target_pairs={{4,0},{8,4},{12,8},{0,12},{5,1},{9,5},{13,9},{1,13},{6,2},{10,6},{... | collective-permute-start | bytes 18440 | tf_op jit(solution)/shard_map/ppermute | solution.py:38
  8.4 2.3 copy-start.9
  8.5 2.1 copy-start.13
  13.0 1.0 copy-start.7
  13.0 7.2 %copy-start.15 = (s32[16,16]{1,0:T(8,128)S(1)}, s32[16,16]{1,0:T(8,128)}, u32[]{:S(2)}) copy-start(s32[16,16]{1,0:T(8,128)} %param.21) | copy-start | bytes 3076
  14.9 10.1 %collective-permute-start.4 = (bf16[18,64,128]{2,1,0:T(8,128)(2,1)}, bf16[18,64,128]{2,1,0:T(8,128)(2,1)}, u32[]{:S(2)}, u32[]{:S(2)}) collective-permute-start(bf16[18,64,128]{2,1,0:T(8,128)(2,1)} %get-tuple-element.15), channel_id=1, source_target_pairs={{4,0},{8,4},{12,8},{5,1},{9,5},{13,9},{6,2},{10,6},{14,10},{7,3},{... | collective-permute-start | bytes 884744 | tf_op jit(solution)/shard_map/ppermute | solution.py:30
  17.9 10.0 %collective-permute-start.3 = (bf16[18,64,128]{2,1,0:T(8,128)(2,1)}, bf16[18,64,128]{2,1,0:T(8,128)(2,1)}, u32[]{:S(2)}, u32[]{:S(2)}) collective-permute-start(bf16[18,64,128]{2,1,0:T(8,128)(2,1)} %get-tuple-element.16), channel_id=1, source_target_pairs={{0,4},{4,8},{8,12},{1,5},{5,9},{9,13},{2,6},{6,10},{10,14},{3,7},{... | collective-permute-start | bytes 884744 | tf_op jit(solution)/shard_map/ppermute | solution.py:28
  20.4 4.5 %copy-start.12 = (bf16[3,64,128]{2,1,0:T(8,128)(2,1)S(1)}, bf16[3,64,128]{2,1,0:T(8,128)(2,1)}, u32[]{:S(2)}) copy-start(bf16[3,64,128]{2,1,0:T(8,128)(2,1)} %param.16) | copy-start | bytes 147460
  25.0 5.3 %copy-start.6 = (bf16[128,64,64]{1,0,2:T(8,128)(2,1)S(1)}, bf16[128,64,64]{1,0,2:T(8,128)(2,1)}, u32[]{:S(2)}) copy-start(bf16[128,64,64]{1,0,2:T(8,128)(2,1)} %copy.58) | copy-start | bytes 3145732
  25.0 22.1 %collective-permute-start = (bf16[47,3,64]{0,2,1:T(8,128)(2,1)S(1)}, bf16[47,3,64]{0,2,1:T(8,128)(2,1)S(1)}, u32[]{:S(2)}, u32[]{:S(2)}) collective-permute-start(bf16[47,3,64]{0,2,1:T(8,128)(2,1)S(1)} %get-tuple-element.21), channel_id=1, source_target_pairs={{0,4},{4,8},{8,12},{1,5},{5,9},{9,13},{2,6},{6,10},{10,14},{3,7},{... | collective-permute-start | bytes 54152 | tf_op jit(solution)/shard_map/ppermute | solution.py:28
  30.3 2.4 copy-start.2
  30.4 3.6 %copy-start.11 = (bf16[64,64,128]{2,1,0:T(8,128)(2,1)S(1)}, bf16[64,64,128]{2,1,0:T(8,128)(2,1)}, u32[]{:S(2)}) copy-start(bf16[64,64,128]{2,1,0:T(8,128)(2,1)} %param.15) | copy-start | bytes 3145732
  32.8 2.6 %copy-start.16 = (s32[16,128]{1,0:T(8,128)S(1)}, s32[16,128]{1,0:T(8,128)}, u32[]{:S(2)}) copy-start(s32[16,128]{1,0:T(8,128)} %param.20) | copy-start | bytes 24580
  32.8 23.3 %collective-permute-start.5 = (bf16[64,64,64]{2,1,0:T(8,128)(2,1)}, bf16[64,64,64]{2,1,0:T(8,128)(2,1)}, u32[]{:S(2)}, u32[]{:S(2)}) collective-permute-start(bf16[64,64,64]{2,1,0:T(8,128)(2,1)} %get-tuple-element.23), channel_id=1, source_target_pairs={{2,0},{0,2},{3,1},{1,3},{6,4},{4,6},{7,5},{5,7},{10,8},{8,10},{11,... | collective-permute-start | bytes 1572872 | tf_op jit(solution)/shard_map/ppermute | solution.py:38
  38.4 8.8 %collective-permute-start.1 = (bf16[47,3,64]{0,2,1:T(8,128)(2,1)S(1)}, bf16[47,3,64]{0,2,1:T(8,128)(2,1)S(1)}, u32[]{:S(2)}, u32[]{:S(2)}) collective-permute-start(bf16[47,3,64]{0,2,1:T(8,128)(2,1)S(1)} %get-tuple-element.22), channel_id=1, source_target_pairs={{4,0},{8,4},{12,8},{5,1},{9,5},{13,9},{6,2},{10,6},{14,10},{7,3},{... | collective-permute-start | bytes 54152 | tf_op jit(solution)/shard_map/ppermute | solution.py:30
  41.1 20.3 %collective-permute-start.17 = (bf16[18,3,256]{2,1,0:T(4,128)(2,1)}, bf16[18,3,256]{2,1,0:T(4,128)(2,1)}, u32[]{:S(2)}, u32[]{:S(2)}) collective-permute-start(bf16[18,3,256]{2,1,0:T(4,128)(2,1)} %get-tuple-element.19), channel_id=1, source_target_pairs={{4,0},{8,4},{12,8},{5,1},{9,5},{13,9},{6,2},{10,6},{14,10},{7,3},{... | collective-permute-start | bytes 82952 | tf_op jit(solution)/shard_map/ppermute | solution.py:30
  43.0 18.4 %collective-permute-start.16 = (bf16[18,3,256]{2,1,0:T(4,128)(2,1)}, bf16[18,3,256]{2,1,0:T(4,128)(2,1)}, u32[]{:S(2)}, u32[]{:S(2)}) collective-permute-start(bf16[18,3,256]{2,1,0:T(4,128)(2,1)} %get-tuple-element.20), channel_id=1, source_target_pairs={{0,4},{4,8},{8,12},{1,5},{5,9},{9,13},{2,6},{6,10},{10,14},{3,7},{... | collective-permute-start | bytes 82952 | tf_op jit(solution)/shard_map/ppermute | solution.py:28
  58.3 3.1 %copy-start.10 = (bf16[3,256,128]{1,0,2:T(4,128)(2,1)S(1)}, bf16[3,256,128]{1,0,2:T(4,128)(2,1)}, u32[]{:S(2)}) copy-start(bf16[3,256,128]{1,0,2:T(4,128)(2,1)} %copy-done.9) | copy-start | bytes 589828
  58.3 4.2 %copy-start.3 = (bf16[100,64,128]{2,1,0:T(8,128)(2,1)S(1)}, bf16[100,64,128]{2,1,0:T(8,128)(2,1)}, u32[]{:S(2)}) copy-start(bf16[100,64,128]{2,1,0:T(8,128)(2,1)} %copy-done.2) | copy-start | bytes 4915204
  58.8 5.7 %collective-permute-start.12 = (bf16[8,64,64]{2,1,0:T(8,128)(2,1)S(1)}, bf16[8,64,64]{2,1,0:T(8,128)(2,1)S(1)}, u32[]{:S(2)}, u32[]{:S(2)}) collective-permute-start(bf16[8,64,64]{2,1,0:T(8,128)(2,1)S(1)} %convolution_convert_fusion), channel_id=1, source_target_pairs={{1,0},{0,1},{3,2},{2,3},{5,4},{4,5},{7,6},{6,7},{9,8},{8,9},{11,10... | collective-permute-start | bytes 196616 | tf_op jit(solution)/shard_map/ppermute | solution.py:38
  62.5 48.8 %collective-permute-start.18 = (bf16[100,64,128]{2,1,0:T(8,128)(2,1)S(1)}, bf16[100,64,128]{2,1,0:T(8,128)(2,1)S(1)}, u32[]{:S(2)}, u32[]{:S(2)}) collective-permute-start(bf16[100,64,128]{2,1,0:T(8,128)(2,1)S(1)} %copy-done.3), channel_id=1, source_target_pairs={{2,0},{0,2},{3,1},{1,3},{6,4},{4,6},{7,5},{5,7},{10,8},{8,10},{11,... | collective-permute-start | bytes 4915208 | tf_op jit(solution)/shard_map/ppermute | solution.py:38
  63.8 2.9 %collective-permute-start.6 = (bf16[64,64,64]{2,1,0:T(8,128)(2,1)S(1)}, bf16[64,64,64]{2,1,0:T(8,128)(2,1)S(1)}, u32[]{:S(2)}, u32[]{:S(2)}) collective-permute-start(bf16[64,64,64]{2,1,0:T(8,128)(2,1)S(1)} %add_convert_fusion), channel_id=1, source_target_pairs={{1,0},{0,1},{3,2},{2,3},{5,4},{4,5},{7,6},{6,7},{9,8},{8,9},{11,10... | collective-permute-start | bytes 1572872 | tf_op jit(solution)/shard_map/ppermute | solution.py:38
  64.6 19.7 %collective-permute-start.14 = (bf16[16,64,64]{2,1,0:T(8,128)(2,1)S(1)}, bf16[16,64,64]{2,1,0:T(8,128)(2,1)S(1)}, u32[]{:S(2)}, u32[]{:S(2)}) collective-permute-start(bf16[16,64,64]{2,1,0:T(8,128)(2,1)S(1)} %pad_maximum_fusion.3), channel_id=1, source_target_pairs={{8,0},{12,4},{0,8},{4,12},{9,1},{13,5},{1,9},{5,13},{10,2},{14,6},... | collective-permute-start | bytes 393224 | tf_op jit(solution)/shard_map/ppermute | solution.py:38
  65.3 19.1 %collective-permute-start.13 = (bf16[16,64,64]{2,1,0:T(8,128)(2,1)S(1)}, bf16[16,64,64]{2,1,0:T(8,128)(2,1)S(1)}, u32[]{:S(2)}, u32[]{:S(2)}) collective-permute-start(bf16[16,64,64]{2,1,0:T(8,128)(2,1)S(1)} %pad_maximum_fusion.3), channel_id=1, source_target_pairs={{4,0},{8,4},{12,8},{0,12},{5,1},{9,5},{13,9},{1,13},{6,2},{10,6},{... | collective-permute-start | bytes 393224 | tf_op jit(solution)/shard_map/ppermute | solution.py:38
  67.0 37.5 %collective-permute-start.7 = (bf16[47,64,64]{2,1,0:T(8,128)(2,1)S(1)}, bf16[47,64,64]{2,1,0:T(8,128)(2,1)S(1)}, u32[]{:S(2)}, u32[]{:S(2)}) collective-permute-start(bf16[47,64,64]{2,1,0:T(8,128)(2,1)S(1)} %slice.43), channel_id=1, source_target_pairs={{0,4},{4,8},{8,12},{1,5},{5,9},{9,13},{2,6},{6,10},{10,14},{3,7},{... | collective-permute-start | bytes 1155080 | tf_op jit(solution)/shard_map/ppermute | solution.py:28
  68.9 37.5 %collective-permute-start.8 = (bf16[47,64,64]{2,1,0:T(8,128)(2,1)S(1)}, bf16[47,64,64]{2,1,0:T(8,128)(2,1)S(1)}, u32[]{:S(2)}, u32[]{:S(2)}) collective-permute-start(bf16[47,64,64]{2,1,0:T(8,128)(2,1)S(1)} %slice.44), channel_id=1, source_target_pairs={{4,0},{8,4},{12,8},{5,1},{9,5},{13,9},{6,2},{10,6},{14,10},{7,3},{... | collective-permute-start | bytes 1155080 | tf_op jit(solution)/shard_map/ppermute | solution.py:30
  84.3 20.1 %collective-permute-start.15 = (bf16[16,64,64]{2,1,0:T(8,128)(2,1)S(1)}, bf16[16,64,64]{2,1,0:T(8,128)(2,1)S(1)}, u32[]{:S(2)}, u32[]{:S(2)}) collective-permute-start(bf16[16,64,64]{2,1,0:T(8,128)(2,1)S(1)} %pad_maximum_fusion.3), channel_id=1, source_target_pairs={{12,0},{0,4},{4,8},{8,12},{13,1},{1,5},{5,9},{9,13},{14,2},{2,6},{... | collective-permute-start | bytes 393224 | tf_op jit(solution)/shard_map/ppermute | solution.py:38
  104.5 6.9 %copy-start.4 = (bf16[26,16,256]{2,1,0:T(8,128)(2,1)S(1)}, bf16[26,16,256]{2,1,0:T(8,128)(2,1)}, u32[]{:S(2)}) copy-start(bf16[26,16,256]{2,1,0:T(8,128)(2,1)} %constant.115.clone.added_ref) | copy-start | bytes 638980
  104.5 6.9 %copy-start.5 = (bf16[26,16,256]{2,1,0:T(8,128)(2,1)S(1)}, bf16[26,16,256]{2,1,0:T(8,128)(2,1)}, u32[]{:S(2)}) copy-start(bf16[26,16,256]{2,1,0:T(8,128)(2,1)} %constant.114.clone.factor_ref) | copy-start | bytes 638980
  228.9 1.3 copy-start.1
  234.6 2.0 collective-permute-start.19

commit v2 on v1

--- a/solution.py
+++ b/solution.py
@@ -11,6 +11,7 @@
 STRIP = 8
 GROUP = 4
 FEATURES = 16
+NEAR_CALLS = 2
 
 softening = 0.25
 spacing = 16.0
@@ -18,19 +19,19 @@
 far_power = 256.0
 
 
-def padded(cells, axis, width):
-    count = lax.axis_size(axis)
-    ends = count - 1
+def halo(cells, axis, width):
+    ends = lax.axis_size(axis) - 1
     head = cells[:width]
     tail = cells[cells.shape[0] - width :]
-    return jnp.concatenate(
-        [
-            lax.ppermute(tail, axis, [(i, i + 1) for i in range(ends)]),
-            cells,
-            lax.ppermute(head, axis, [(i + 1, i) for i in range(ends)]),
-        ],
-        axis=0,
-    )
+    return [
+        lax.ppermute(tail, axis, [(i, i + 1) for i in range(ends)]),
+        cells,
+        lax.ppermute(head, axis, [(i + 1, i) for i in range(ends)]),
+    ]
+
+
+def padded(cells, axis, width):
+    return jnp.concatenate(halo(cells, axis, width), axis=0)
 
 
 def rotated(cells, axis, step):
@@ -97,6 +98,8 @@
 def near_kernel(
     slots,
     shares,
+    first_border,
+    border_count,
     codes_ref,
     groups_ref,
     own_ref,
@@ -114,7 +117,7 @@
         base_ref[j] = column_features(border_ref[j], near_power, True).astype(jnp.bfloat16)
         return 0
 
-    lax.fori_loop(0, border_ref.shape[0], base_step, 0, unroll=2)
+    lax.fori_loop(first_border, first_border + border_count, base_step, 0, unroll=2)
 
     def row_step(i, at):
         rows_ref[i] = jnp.transpose(row_features(own_ref[i])).astype(jnp.bfloat16)
@@ -139,7 +142,7 @@
             code = codes_ref[start + u]
             column = base_ref[code // 32] * factor_ref[code % 32] + added_ref[code % 32]
             square = jnp.dot(row, column, preferred_element_type=jnp.float32)
-            tiles_ref[slot, :, u * width : (u + 1) * width] = lax.rsqrt(square).astype(jnp.bfloat16)
+            tiles_ref[slot, :, u * width : (u + 1) * width] = lax.rsqrt(square.astype(jnp.bfloat16))
 
     def sum_stage(at, slot):
         start = code_at[at]
@@ -181,12 +184,14 @@
     parent_moments_ref,
     transfer_ref,
     basis_ref,
-    near_ref,
-    out_ref,
-    leaf_cols_ref,
-    parent_cols_ref,
+    *refs,
 ):
-    parents = out_ref.shape[0] // STRIP
+    near_refs = refs[:NEAR_CALLS]
+    out_ref, leaf_cols_ref, parent_cols_ref, rows_ref, tiles_ref, parent_field_ref, field_ref = refs[
+        NEAR_CALLS:
+    ]
+    leaves = out_ref.shape[0]
+    parents = leaves // STRIP
 
     def fill(skeleton_ref, cols_ref):
         def step(j, _):
@@ -194,57 +199,80 @@
             cols_ref[j] = jnp.transpose(columns).astype(jnp.bfloat16)
             return 0
 
-        lax.fori_loop(0, skeleton_ref.shape[0], step, 0, unroll=2)
+        lax.fori_loop(0, skeleton_ref.shape[0], step, 0, unroll=4)
 
     fill(leaf_skeleton_ref, leaf_cols_ref)
     fill(parent_skeleton_ref, parent_cols_ref)
 
-    def coupled(cells, slots, start, ids_ref, cols_ref, moments_ref):
-        row = jnp.transpose(row_features(cells)).astype(jnp.bfloat16)
-        ids = [ids_ref[start + u] for u in range(slots)]
-        column = jnp.concatenate([cols_ref[j] for j in ids], axis=0)
+    def row_step(i, _):
+        rows_ref[i] = jnp.transpose(row_features(leaf_skeleton_ref[leaf_reach + i])).astype(
+            jnp.bfloat16
+        )
+        return 0
+
+    lax.fori_loop(0, leaves, row_step, 0, unroll=4)
+
+    def stacked(slots, start, ids_ref, ref):
+        return jnp.concatenate([ref[ids_ref[start + u]] for u in range(slots)], axis=0)
+
+    def tile_of(row, column):
         square = lax.dot_general(
             row, column, (((1,), (1,)), ((), ())), preferred_element_type=jnp.float32
         )
-        return jnp.dot(
-            lax.rsqrt(square).astype(jnp.bfloat16),
-            jnp.concatenate([moments_ref[j] for j in ids], axis=0),
+        return lax.rsqrt(square).astype(jnp.bfloat16)
+
+    def parent_step(p, _):
+        start = p * parent_slots
+        row = jnp.transpose(row_features(parent_skeleton_ref[own_start_ref[0] + p]))
+        parent_field_ref[p] = jnp.dot(
+            tile_of(
+                row.astype(jnp.bfloat16),
+                stacked(parent_slots, start, parent_ids_ref, parent_cols_ref),
+            ),
+            stacked(parent_slots, start, parent_ids_ref, parent_moments_ref),
             preferred_element_type=jnp.float32,
-        )
-
-    def parent_step(p, _):
-        parent_field = coupled(
-            parent_skeleton_ref[own_start_ref[0] + p],
-            parent_slots,
-            p * parent_slots,
-            parent_ids_ref,
-            parent_cols_ref,
-            parent_moments_ref,
         ).astype(jnp.bfloat16)
-
-        def leaf_step(child, _):
-            i = p * STRIP + child
-            field = coupled(
-                leaf_skeleton_ref[leaf_reach + i],
-                leaf_slots,
-                i * leaf_slots,
-                leaf_ids_ref,
-                leaf_cols_ref,
-                leaf_moments_ref,
-            )
-            leaf_field = field + jnp.dot(
-                transfer_ref[i], parent_field, preferred_element_type=jnp.float32
-            )
-            far = jnp.dot(
-                basis_ref[i], leaf_field.astype(jnp.bfloat16), preferred_element_type=jnp.float32
-            )
-            out_ref[i] = (near_ref[i] + far).astype(out_ref.dtype)
+        return 0
+
+    lax.fori_loop(0, parents, parent_step, 0)
+
+    def tile_stage(i, slot):
+        tiles_ref[slot] = tile_of(
+            rows_ref[i], stacked(leaf_slots, i * leaf_slots, leaf_ids_ref, leaf_cols_ref)
+        )
+
+    def sum_stage(i, slot):
+        field = jnp.dot(
+            tiles_ref[slot],
+            stacked(leaf_slots, i * leaf_slots, leaf_ids_ref, leaf_moments_ref),
+            preferred_element_type=jnp.float32,
+        )
+        spread = jnp.dot(
+            transfer_ref[i], parent_field_ref[i // STRIP], preferred_element_type=jnp.float32
+        )
+        field_ref[i] = (field + spread).astype(jnp.bfloat16)
+
+    tile_stage(0, 0)
+
+    def pair_step(t, _):
+        tile_stage(2 * t + 1, 1)
+        sum_stage(2 * t, 0)
+        tile_stage(jnp.minimum(2 * t + 2, leaves - 1), 0)
+        sum_stage(2 * t + 1, 1)
+        return 0
+
+    lax.fori_loop(0, leaves // 2, pair_step, 0)
+
+    share = leaves // NEAR_CALLS
+    for part, near_ref in enumerate(near_refs):
+
+        def last_step(k, _):
+            i = part * share + k
+            far = jnp.dot(basis_ref[i], field_ref[i], preferred_element_type=jnp.float32)
+            out_ref[i] = jnp.transpose(near_ref[k] + far).astype(out_ref.dtype)
             return 0
 
-        lax.fori_loop(0, STRIP, leaf_step, 0, unroll=4)
-        return 0
-
-    lax.fori_loop(0, parents, parent_step, 0)
+        lax.fori_loop(0, share, last_step, 0, unroll=4)
 
 
 def in_smem(count):
@@ -306,13 +334,45 @@
         (listing % STRIP - row_ids[None, :] % STRIP + 2)
         + 5 * (listing // STRIP - row_ids[None, :] // STRIP + 2)
     )
-    code = jnp.where(live, (listing - (first_leaf - near_reach)) * 32 + offset, 25)
+    share = own // NEAR_CALLS
+    idle = jnp.arange(own, dtype=jnp.int32) // share * share * 32 + 25
+    code = jnp.where(live, (listing - (first_leaf - near_reach)) * 32 + offset, idle[None, :])
     slots = -(-near_list.shape[0] // GROUP) * GROUP
-    code = jnp.pad(
-        jnp.transpose(code), ((0, 1), (0, slots - near_list.shape[0])), constant_values=25
-    ).reshape(-1)
+    spare = jnp.broadcast_to(idle[:, None], (own, slots - near_list.shape[0]))
+    code = jnp.concatenate([jnp.transpose(code), spare], axis=1).reshape(-1)
     groups = (counts + (GROUP - 1)) // GROUP
     factor, added = offset_tables(border_points.shape[2])
+
+    def near_call(part, after):
+        share = own // NEAR_CALLS
+        first = part * share
+        cut = lambda array, start, width: lax.slice_in_dim(array, start, start + width, axis=0)
+        part_codes = jnp.concatenate(
+            [
+                cut(code, first * slots, share * slots),
+                jnp.full((slots,), first * 32 + 25, jnp.int32),
+            ]
+        )
+        part_groups, after = lax.optimization_barrier((cut(groups, first, share), after))
+        field = pl.pallas_call(
+            functools.partial(near_kernel, slots, near_parts, first, share + 2 * near_reach),
+            out_shape=jax.ShapeDtypeStruct((share, rows_here, all_columns), jnp.float32),
+            in_specs=in_smem(2) + in_vmem(4 + near_parts),
+            out_specs=pl.BlockSpec(memory_space=pltpu.VMEM),
+            scratch_shapes=[
+                pltpu.VMEM((window, FEATURES, border_points.shape[2]), jnp.bfloat16),
+                pltpu.VMEM((share, rows_here, FEATURES), jnp.bfloat16),
+                pltpu.VMEM((2, rows_here, GROUP * border_points.shape[2]), jnp.bfloat16),
+                pltpu.SMEM((share * (slots // GROUP) + 3,), jnp.int32),
+                pltpu.SMEM((share * (slots // GROUP) + 3,), jnp.int32),
+            ],
+            compiler_params=pltpu.CompilerParams(vmem_limit_bytes=48 * 2**20),
+            cost_estimate=pl.CostEstimate(
+                flops=30 * 10**9, bytes_accessed=16 * 10**6, transcendentals=0
+            ),
+            name="near_field",
+        )(part_codes, part_groups, cut(own_points, first, share), border_points, factor, added, *shares)
+        return field, after
 
     basis_cells = jnp.transpose(mine(basis, 2), (2, 0, 1))
     own_charges = lax.slice_in_dim(wide, near_reach, near_reach + own, axis=0)
@@ -320,8 +380,11 @@
         "isa,ics->iac", basis_cells, own_charges, preferred_element_type=jnp.float32
     )
     sent = partial.astype(jnp.bfloat16)
-    for k in range(1, near_parts):
-        partial = partial + rotated(sent, "near", k).astype(jnp.float32)
+    arrived = [rotated(sent, "near", k) for k in range(1, near_parts)]
+    near_first, partial = near_call(0, partial)
+    near_first, arrived = lax.optimization_barrier((near_first, arrived))
+    for other in arrived:
+        partial = partial + other.astype(jnp.float32)
     moments0 = partial.astype(jnp.bfloat16)
     transfer_cells = jnp.transpose(mine(transfer, 2), (2, 0, 1))
     moments1 = jnp.einsum(
@@ -331,36 +394,21 @@
         preferred_element_type=jnp.float32,
     ).astype(jnp.bfloat16)
     chip_parents = paired(moments1, rhs_index, 0)
-    turn = lambda cells: jnp.concatenate(
-        [cells] + [rotated(cells, "leaf", k) for k in range(1, leaf_parts)], axis=0
-    )
-    every_moments = turn(chip_parents)
+    turned = lambda cells: [cells] + [rotated(cells, "leaf", k) for k in range(1, leaf_parts)]
+    every_moments = turned(chip_parents)
     chip_moments = paired(moments0, rhs_index, 0)
-    border_moments = mine(padded(chip_moments, "leaf", far_reach), 0, own + 2 * far_reach)
-
-    near_part = pl.pallas_call(
-        functools.partial(near_kernel, slots, near_parts),
-        out_shape=jax.ShapeDtypeStruct((own, rows_here, all_columns), jnp.float32),
-        in_specs=in_smem(2) + in_vmem(4 + near_parts),
-        out_specs=pl.BlockSpec(memory_space=pltpu.VMEM),
-        scratch_shapes=[
-            pltpu.VMEM((window, FEATURES, border_points.shape[2]), jnp.bfloat16),
-            pltpu.VMEM((own, rows_here, FEATURES), jnp.bfloat16),
-            pltpu.VMEM((2, rows_here, GROUP * border_points.shape[2]), jnp.bfloat16),
-            pltpu.SMEM((own * (slots // GROUP) + 3,), jnp.int32),
-            pltpu.SMEM((own * (slots // GROUP) + 3,), jnp.int32),
-        ],
-        compiler_params=pltpu.CompilerParams(vmem_limit_bytes=48 * 2**20),
-        cost_estimate=pl.CostEstimate(
-            flops=60 * 10**9, bytes_accessed=16 * 10**6, transcendentals=0
-        ),
-        name="near_field",
-    )(code, groups, own_points, border_points, factor, added, *shares)
+    border_moments = halo(chip_moments, "leaf", far_reach)
+    near_second, chip_moments = near_call(1, chip_moments)
+    near_second, every_moments, border_moments = lax.optimization_barrier(
+        (near_second, every_moments, border_moments)
+    )
+    every_moments = jnp.concatenate(every_moments, axis=0)
+    border_moments = mine(jnp.concatenate(border_moments, axis=0), 0, own + 2 * far_reach)
 
     skeleton_cells = jnp.transpose(leaf_skeleton, (2, 0, 1))
     border_skeleton = mine(padded(skeleton_cells, "leaf", far_reach), 0, own + 2 * far_reach)
     parent_cells = jnp.transpose(parent_skeleton, (2, 0, 1))
-    every_skeleton = turn(parent_cells)
+    every_skeleton = jnp.concatenate(turned(parent_cells), axis=0)
     parent_start = rhs_index * own_parents
     leaf_ids = jnp.transpose(mine(leaf_far, 1) - (first_leaf - far_reach)).reshape(-1)
     chip_count = parent_far.shape[1]
@@ -369,12 +417,16 @@
 
     result = pl.pallas_call(
         functools.partial(far_kernel, leaf_far.shape[0], parent_far.shape[0], far_reach),
-        out_shape=jax.ShapeDtypeStruct((own, rows_here, all_columns), jnp.bfloat16),
-        in_specs=in_smem(3) + in_vmem(7),
+        out_shape=jax.ShapeDtypeStruct((own, all_columns, rows_here), jnp.bfloat16),
+        in_specs=in_smem(3) + in_vmem(6 + NEAR_CALLS),
         out_specs=pl.BlockSpec(memory_space=pltpu.VMEM),
         scratch_shapes=[
             pltpu.VMEM((own + 2 * far_reach, rank_size, FEATURES), jnp.bfloat16),
             pltpu.VMEM((leaf_parts * chip_count, rank_size, FEATURES), jnp.bfloat16),
+            pltpu.VMEM((own, rank_size, FEATURES), jnp.bfloat16),
+            pltpu.VMEM((2, rank_size, leaf_far.shape[0] * rank_size), jnp.bfloat16),
+            pltpu.VMEM((own_parents, rank_size, all_columns), jnp.bfloat16),
+            pltpu.VMEM((own, rank_size, all_columns), jnp.bfloat16),
         ],
         compiler_params=pltpu.CompilerParams(vmem_limit_bytes=48 * 2**20),
         name="far_field",
@@ -388,16 +440,17 @@
         every_moments,
         transfer_cells,
         basis_cells,
-        near_part,
-    )
-    result = jnp.transpose(result, (1, 2, 0))
+        near_first,
+        near_second,
+    )
     kept = mine(result, 1, columns, rhs_index * columns)
     given = mine(result, 1, columns, (1 - rhs_index) * columns)
     taken = rotated(given, "rhs", 1)
     first = rhs_index == 0
-    return jnp.concatenate(
-        [jnp.where(first, kept, taken), jnp.where(first, taken, kept)], axis=2
-    )
+    result = jnp.concatenate(
+        [jnp.where(first, kept, taken), jnp.where(first, taken, kept)], axis=0
+    )
+    return jnp.transpose(result, (2, 1, 0))
 
 
 def solution(mesh):

time: 255 us -> 217 us (0.85)
  waiting for transfers between devices: 43.1 us -> 14 us
  Pallas kernels: 118 us -> 107 us
  starting transfers between devices: 33.3 us -> 39.7 us
  local copies, waits for them, and re-layouts: 32.8 us -> 26.8 us
  other arithmetic: 24.4 us -> 21 us
    ppermute x12, waiting for transfers between devices: 41.1 us -> 11.5 us  [rotated(): lax.ppermute(cells, axis, [((i + step) % count, i) for i in range(count)])]
    pallas_call x1, Pallas kernels: 42.8 us -> 30 us  [per_device(): pl.pallas_call(functools.partial(far_kernel, leaf_far.shape[0], parent_fa...]
    select_n x2 -> x0, local copies, waits for them, and re-layouts: 7.42 us -> none  [the longest x1 4.09 us: per_device(): jnp.where(first, taken, kept)]
    ppermute x12, starting transfers between devices: 12 us -> 17.8 us  [rotated(): lax.ppermute(cells, axis, [((i + step) % count, i) for i in range(count)])]
    select_n x1, other arithmetic: 5.87 us -> 1.26 us  [per_device(): jnp.where(first, kept, taken)]
    dynamic_slice x4 -> x3, local copies, waits for them, and re-layouts: 7.79 us -> 3.44 us  [mine(): return lax.dynamic_slice_in_dim(array, start, width, dim)]
    concatenate x5 -> x6, other arithmetic: 12 us -> 9.07 us  [the longest x3 5.72 us: padded(): return jnp.concatenate(halo(cells, axis, width), axis=0)]
    pallas_call x1 -> x2, Pallas kernels: 74.7 us -> 77.1 us  [near_call(): pl.pallas_call(functools.partial(near_kernel, slots, near_parts, first, s...]
  transfers between devices with their start and end apart: 20 -> 20, of which waited for: 6 -> 4; matrix products, arithmetic and copies ran while one was open for 13% -> 19% of each run, Pallas kernels for 0% -> 36%
where the time goes in v2:
time: 217 us; the launch traced here: 214 us
  Pallas kernels  107 us (49%)
  starting transfers between devices  39.7 us (18%)
  local copies, waits for them, and re-layouts  26.8 us (12%)
  other arithmetic  21 us (10%)
  waiting for transfers between devices  14 us (6%)
  matrix products  4.99 us (2%)
    pallas_call x2, Pallas kernels, near_call(): pl.pallas_call(functools.partial(near_kernel, slots, near_parts, first, s...  77.1 us
    pallas_call x1, Pallas kernels, per_device(): pl.pallas_call(functools.partial(far_kernel, leaf_far.shape[0], parent_fa...  30 us
    ppermute x12, starting transfers between devices, rotated(): lax.ppermute(cells, axis, [((i + step) % count, i) for i in range(count)])  17.8 us
    unnamed x54, local copies, waits for them, and re-layouts  16.5 us
    ppermute x4, starting transfers between devices, halo(): lax.ppermute(head, axis, [(i + 1, i) for i in range(ends)])  12.2 us
    ppermute x12, waiting for transfers between devices, rotated(): lax.ppermute(cells, axis, [((i + step) % count, i) for i in range(count)])  11.5 us
    ppermute x4, starting transfers between devices, halo(): lax.ppermute(tail, axis, [(i, i + 1) for i in range(ends)])  9.76 us
    concatenate x3, other arithmetic, padded(): return jnp.concatenate(halo(cells, axis, width), axis=0)  5.72 us
  transfers between devices with their start and end apart: 20, of which 4 were waited for; matrix products, arithmetic and copies ran while one was open for 19% of the time, Pallas kernels for 36%

profile of v2, /device:TPU:13, one launch (start us, length us, event | category | flops | bytes accessed | tf_op | source)
XLA Modules:
  0.0 214.2 jit_solution(291464574415931630)
XLA Ops:
  0.9 1.3 collective-permute-start.18
  2.2 1.1 collective-permute-start.17
  3.3 1.4 collective-permute-start.16
  4.7 2.5 %copy.43 = bf16[128,32,128]{0,1,2:T(8,128)(2,1)S(1)} copy(bf16[128,32,128]{2,1,0:T(8,128)(2,1)} %param.13) | data formatting | bytes 2097152 | tf_op args[1]
  7.1 1.6 collective-permute-start.2
  9.1 2.0 constant_dynamic-slice_fusion.2
  11.7 1.7 broadcast_select_fusion.1
  13.4 0.9 copy-done.15
  14.4 0.9 pad_maximum_fusion.2
  15.3 1.9 collective-permute-start.3
  17.2 4.1 %collective-permute-start.4 = (bf16[18,64,128]{2,1,0:T(8,128)(2,1)}, bf16[18,64,128]{2,1,0:T(8,128)(2,1)}, u32[]{:S(2)}, u32[]{:S(2)}) collective-permute-start(bf16[18,64,128]{2,1,0:T(8,128)(2,1)} %get-tuple-element.35), channel_id=1, source_target_pairs={{4,0},{8,4},{12,8},{5,1},{9,5},{13,9},{6,2},{10,6},{14,10},{7,3},{... | collective-permute-start | bytes 884744 | tf_op jit(solution)/shard_map/ppermute | solution.py:29
  21.3 1.4 constant_dynamic-slice_fusion.1
  22.7 1.1 copy.46
  24.5 1.6 collective-permute-done.3
  26.1 2.0 collective-permute-start.1
  28.2 3.6 %fusion.3.refs_0_ = bf16[100,64,128]{2,1,0:T(8,128)(2,1)} fusion(s32[]{:T(128)S(6)} %select_n.152, bf16[18,64,128]{2,1,0:T(8,128)(2,1)} %collective-permute-done.3, bf16[128,32,128]{2,1,0:T(8,128)(2,1)S(1)} %get-tuple-element.37, bf16[128,32,128]{2,1,0:T(8,128)(2,1)} %copy-done.15, bf16[18,64,128]{2,1,0:T(8,128)(2,1)} %collective-permute-done.4), kind=kLoop, calls=%fused_computation.12 | loop fusion | flops 6553600 | bytes 4325380 | tf_op jit(solution)/shard_map/concatenate | solution.py:34
  31.8 1.2 collective-permute-start.7
  34.8 4.5 %copy.56 = bf16[128,64,64]{1,0,2:T(8,128)(2,1)} copy(bf16[128,64,64]{2,1,0:T(8,128)(2,1)} %constant_dynamic-slice_fusion.2) | data formatting | bytes 2097152
  39.4 2.6 %copy.57 = bf16[64,64,64]{1,0,2:T(8,128)(2,1)S(1)} copy(bf16[64,64,64]{2,1,0:T(8,128)(2,1)} %constant_dynamic-slice_fusion.1) | data formatting | bytes 1048576
  43.2 3.4 %collective-permute-start = (bf16[47,3,64]{0,2,1:T(8,128)(2,1)}, bf16[47,3,64]{0,2,1:T(8,128)(2,1)S(1)}, u32[]{:S(2)}, u32[]{:S(2)}) collective-permute-start(bf16[47,3,64]{0,2,1:T(8,128)(2,1)} %get-tuple-element.47), channel_id=1, source_target_pairs={{0,4},{4,8},{8,12},{1,5},{5,9},{9,13},{2,6},{6,10},{10,14},{3,7},{... | collective-permute-start | bytes 54152 | tf_op jit(solution)/shard_map/ppermute | solution.py:27
  46.6 2.6 %collective-permute-start.5 = (bf16[18,3,256]{2,1,0:T(4,128)(2,1)S(1)}, bf16[18,3,256]{2,1,0:T(4,128)(2,1)S(1)}, u32[]{:S(2)}, u32[]{:S(2)}) collective-permute-start(bf16[18,3,256]{2,1,0:T(4,128)(2,1)S(1)} %get-tuple-element.46), channel_id=1, source_target_pairs={{0,4},{4,8},{8,12},{1,5},{5,9},{9,13},{2,6},{6,10},{10,14},{3,7},{... | collective-permute-start | bytes 82952 | tf_op jit(solution)/shard_map/ppermute | solution.py:27
  49.2 2.7 %collective-permute-start.6 = (bf16[18,3,256]{2,1,0:T(4,128)(2,1)S(1)}, bf16[18,3,256]{2,1,0:T(4,128)(2,1)S(1)}, u32[]{:S(2)}, u32[]{:S(2)}) collective-permute-start(bf16[18,3,256]{2,1,0:T(4,128)(2,1)S(1)} %get-tuple-element.45), channel_id=1, source_target_pairs={{4,0},{8,4},{12,8},{5,1},{9,5},{13,9},{6,2},{10,6},{14,10},{7,3},{... | collective-permute-start | bytes 82952 | tf_op jit(solution)/shard_map/ppermute | solution.py:29
  51.9 1.5 maximum_convert_fusion.parent_skeleton_ref
  53.4 0.9 collective-permute-done.6
  55.7 2.6 %fusion.32 = (bf16[64,64,64]{2,1,0:T(8,128)(2,1)S(1)}, f32[64,64,64]{2,1,0:T(8,128)S(1)}) fusion(bf16[100,64,128]{2,1,0:T(8,128)(2,1)} %fusion.3.refs_0_, bf16[128,64,64]{1,0,2:T(8,128)(2,1)} %copy.56), kind=kOutput, calls=%fused_computation.95 | convolution fusion | flops 67371008 | bytes 4718592 | tf_op jit(solution)/shard_map/isa,ics->iac/dot_general | solution.py:379
  58.7 9.9 %collective-permute-done.7.refs_1_ = bf16[100,64,128]{2,1,0:T(8,128)(2,1)} collective-permute-done((bf16[100,64,128]{2,1,0:T(8,128)(2,1)}, bf16[100,64,128]{2,1,0:T(8,128)(2,1)}, u32[]{:S(2)}, u32[]{:S(2)}) %collective-permute-start.7) | collective-permute-done | bytes 1638432 | tf_op jit(solution)/shard_map/ppermute | solution.py:39
  68.6 39.6 %near_field.2.refs_0_ = f32[32,128,64]{2,1,0:T(8,128)} custom-call(s32[924]{0:T(1024)S(1)} %copy-done.7, s32[32]{0:T(128)S(1)} %copy-done.10, f32[32,3,128]{2,1,0:T(4,128)S(1)} %get-tuple-element.42.own_ref, f32[100,3,256]{2,1,0:T(4,128)S(1)} %fusion.10.border_ref, bf16[26,16,256]{2,1,0:T(8,128)(2,1)S(1)} %copy-done.11, bf16[26,16,256]{2,1,0:T(8,128)(2,1)S(1)} %copy-done.13, ...), custom_call_target="tpu_custom_call" | custom-call | flops 30000001024 | bytes 16000000 | tf_op jit(solution)/shard_map/near_field/pallas_call | solution.py:357
  108.2 1.3 add_convert_fusion
  109.5 3.5 %collective-permute-start.9 = (bf16[64,64,64]{2,1,0:T(8,128)(2,1)}, bf16[64,64,64]{2,1,0:T(8,128)(2,1)}, u32[]{:S(2)}, u32[]{:S(2)}) collective-permute-start(bf16[64,64,64]{2,1,0:T(8,128)(2,1)} %add_convert_fusion), channel_id=1, source_target_pairs={{1,0},{0,1},{3,2},{2,3},{5,4},{4,5},{7,6},{6,7},{9,8},{8,9},{11,10... | collective-permute-start | bytes 1572872 | tf_op jit(solution)/shard_map/ppermute | solution.py:39
  113.0 2.4 %convolution_convert_fusion = bf16[8,64,64]{2,1,0:T(8,128)(2,1)} fusion(bf16[8,512,64]{2,1,0:T(8,128)(2,1)S(1)} %bitcast.29, bf16[8,512,64]{2,1,0:T(8,128)(2,1)} %bitcast.10), kind=kOutput, calls=%fused_computation.14 | convolution fusion | flops 33587200 | bytes 1114112 | tf_op jit(solution)/shard_map/pkb,pkc->pbc/dot_general | solution.py:390
  115.4 1.6 dynamic-slice_maximum_fusion
  117.0 1.7 copy.55
  118.7 1.0 convert_element_type.21.leaf_skeleton_ref
  119.7 1.0 broadcast_select_fusion.7
  120.8 2.1 collective-permute-start.12
  122.9 2.3 %collective-permute-start.13 = (bf16[16,64,64]{2,1,0:T(8,128)(2,1)S(1)}, bf16[16,64,64]{2,1,0:T(8,128)(2,1)S(1)}, u32[]{:S(2)}, u32[]{:S(2)}) collective-permute-start(bf16[16,64,64]{2,1,0:T(8,128)(2,1)S(1)} %pad_maximum_fusion.4), channel_id=1, source_target_pairs={{12,0},{0,4},{4,8},{8,12},{13,1},{1,5},{5,9},{9,13},{14,2},{2,6},{... | collective-permute-start | bytes 393224 | tf_op jit(solution)/shard_map/ppermute | solution.py:39
  125.2 1.7 broadcast_select_fusion.3
  127.5 1.9 collective-permute-start.14
  129.4 3.4 %collective-permute-start.15 = (bf16[47,64,64]{2,1,0:T(8,128)(2,1)S(1)}, bf16[47,64,64]{2,1,0:T(8,128)(2,1)S(1)}, u32[]{:S(2)}, u32[]{:S(2)}) collective-permute-start(bf16[47,64,64]{2,1,0:T(8,128)(2,1)S(1)} %slice.81), channel_id=1, source_target_pairs={{4,0},{8,4},{12,8},{5,1},{9,5},{13,9},{6,2},{10,6},{14,10},{7,3},{... | collective-permute-start | bytes 1155080 | tf_op jit(solution)/shard_map/ppermute | solution.py:29
  132.9 37.6 %near_field.3.refs_1_ = f32[32,128,64]{2,1,0:T(8,128)} custom-call(s32[924]{0:T(1024)S(1)} %copy-done.6, s32[32]{0:T(128)S(1)} %copy-done.9, f32[32,3,128]{2,1,0:T(4,128)S(1)} %copy-done.4, f32[100,3,256]{2,1,0:T(4,128)S(1)} %fusion.10.border_ref, bf16[26,16,256]{2,1,0:T(8,128)(2,1)S(1)} %copy-done.12, bf16[26,16,256]{2,1,0:T(8,128)(2,1)S(1)} %copy-done.14, ...), custom_call_target="tpu_custom_call" | custom-call | flops 30000001024 | bytes 16000000 | tf_op jit(solution)/shard_map/near_field/pallas_call | solution.py:357
  170.5 3.0 %fusion.1.leaf_moments_ref = bf16[158,64,64]{2,1,0:T(8,128)(2,1)} fusion(s32[]{:T(128)S(6)} %select_n.140, bf16[47,64,64]{2,1,0:T(8,128)(2,1)S(1)} %collective-permute-done.14, bf16[128,64,64]{2,1,0:T(8,128)(2,1)S(1)} %pad_maximum_fusion, bf16[47,64,64]{2,1,0:T(8,128)(2,1)S(1)} %collective-permute-done.15), kind=kLoop, calls=%fused_computation.8 | loop fusion | flops 1294336 | bytes 3112964 | tf_op jit(solution)/shard_map/concatenate | solution.py:406
  173.8 1.3 copy-done.1
  175.1 30.0 %far_field.1 = bf16[64,64,128]{2,1,0:T(8,128)(2,1)S(1)} custom-call(s32[1024]{0:T(1024)S(1)} %copy-done.5, s32[128]{0:T(128)S(1)} %copy-done.8, s32[1]{0:T(128)} %bitcast.2.own_start_ref, f32[158,3,64]{2,1,0:T(4,128)S(1)} %convert_element_type.21.leaf_skeleton_ref, bf16[158,64,64]{2,1,0:T(8,128)(2,1)} %fusion.1.leaf_moments_ref, f32[64,3,64]{2,1,0:T(4,128)S(1)} %copy-done.3, ...), custom_call_target="tpu_custom_call" | custom-call | tf_op jit(solution)/shard_map/far_field/pallas_call | solution.py:418
  205.2 1.0 copy-done.2
  206.2 2.9 %collective-permute-start.19 = (bf16[64,32,128]{2,1,0:T(8,128)(2,1)S(1)}, bf16[64,32,128]{2,1,0:T(8,128)(2,1)S(1)}, u32[]{:S(2)}, u32[]{:S(2)}) collective-permute-start(bf16[64,32,128]{2,1,0:T(8,128)(2,1)S(1)} %constant_dynamic-slice_fusion), channel_id=1, source_target_pairs={{1,0},{0,1},{3,2},{2,3},{5,4},{4,5},{7,6},{6,7},{9,8},{8,9},{11,10... | collective-permute-start | bytes 1572872 | tf_op jit(solution)/shard_map/ppermute | solution.py:39
  209.0 1.5 collective-permute-done.19
  210.6 1.3 broadcast_select_fusion.5
  211.9 2.3 %copy.51 = bf16[128,32,128]{2,1,0:T(8,128)(2,1)} copy(bf16[128,32,128]{0,1,2:T(8,128)(2,1)S(1)} %maximum_bitcast_fusion) | data formatting | bytes 2097152 | tf_op jit(solution)/shard_map/transpose | solution.py:453
  (97 shorter events, 8.5 us)
Async XLA Ops:
  0.0 9.1 %copy-start = (bf16[128,64,128]{2,1,0:T(8,128)(2,1)S(1)}, bf16[128,64,128]{2,1,0:T(8,128)(2,1)}, u32[]{:S(2)}) copy-start(bf16[128,64,128]{2,1,0:T(8,128)(2,1)} %param.14) | copy-start | bytes 6291460
  0.0 8.7 %copy-start.21 = (s32[16,16]{1,0:T(8,128)S(1)}, s32[16,16]{1,0:T(8,128)}, u32[]{:S(2)}) copy-start(s32[16,16]{1,0:T(8,128)} %param.21) | copy-start | bytes 3076
  0.0 9.0 %copy-start.23 = (s32[128]{0:T(128)S(1)}, s32[128]{0:T(128)}, u32[]{:S(2)}) copy-start(s32[128]{0:T(128)} %param.19) | copy-start | bytes 1540
  0.9 42.4 %collective-permute-start.18 = (bf16[16,3,64]{2,1,0:T(4,128)(2,1)S(1)}, bf16[16,3,64]{2,1,0:T(4,128)(2,1)}, u32[]{:S(2)}, u32[]{:S(2)}) collective-permute-start(bf16[16,3,64]{2,1,0:T(4,128)(2,1)S(1)} %bitcast.36), channel_id=1, source_target_pairs={{12,0},{0,4},{4,8},{8,12},{13,1},{1,5},{5,9},{9,13},{14,2},{2,6},{... | collective-permute-start | bytes 18440 | tf_op jit(solution)/shard_map/ppermute | solution.py:39
  2.2 44.4 %collective-permute-start.17 = (bf16[16,3,64]{2,1,0:T(4,128)(2,1)S(1)}, bf16[16,3,64]{2,1,0:T(4,128)(2,1)}, u32[]{:S(2)}, u32[]{:S(2)}) collective-permute-start(bf16[16,3,64]{2,1,0:T(4,128)(2,1)S(1)} %bitcast.37), channel_id=1, source_target_pairs={{8,0},{12,4},{0,8},{4,12},{9,1},{13,5},{1,9},{5,13},{10,2},{14,6},... | collective-permute-start | bytes 18440 | tf_op jit(solution)/shard_map/ppermute | solution.py:39
  3.3 45.9 %collective-permute-start.16 = (bf16[16,3,64]{2,1,0:T(4,128)(2,1)S(1)}, bf16[16,3,64]{2,1,0:T(4,128)(2,1)}, u32[]{:S(2)}, u32[]{:S(2)}) collective-permute-start(bf16[16,3,64]{2,1,0:T(4,128)(2,1)S(1)} %bitcast.38), channel_id=1, source_target_pairs={{4,0},{8,4},{12,8},{0,12},{5,1},{9,5},{13,9},{1,13},{6,2},{10,6},{... | collective-permute-start | bytes 18440 | tf_op jit(solution)/shard_map/ppermute | solution.py:39
  7.1 4.0 %copy-start.16 = (bf16[128,32,128]{0,1,2:T(8,128)(2,1)}, bf16[128,32,128]{0,1,2:T(8,128)(2,1)S(1)}, u32[]{:S(2)}) copy-start(bf16[128,32,128]{0,1,2:T(8,128)(2,1)S(1)} %copy.43) | copy-start | bytes 3145732
  7.1 4.6 %collective-permute-start.2 = (bf16[128,32,128]{2,1,0:T(8,128)(2,1)S(1)}, bf16[128,32,128]{2,1,0:T(8,128)(2,1)}, u32[]{:S(2)}, u32[]{:S(2)}) collective-permute-start(bf16[128,32,128]{2,1,0:T(8,128)(2,1)S(1)} %bitcast.31), channel_id=1, source_target_pairs={{1,0},{0,1},{3,2},{2,3},{5,4},{4,5},{7,6},{6,7},{9,8},{8,9},{11,10... | collective-permute-start | bytes 3145736 | tf_op jit(solution)/shard_map/ppermute | solution.py:39
  9.1 2.6 %copy-start.20 = (s32[25,128]{1,0:T(8,128)S(1)}, s32[25,128]{1,0:T(8,128)}, u32[]{:S(2)}) copy-start(s32[25,128]{1,0:T(8,128)} %param.18) | copy-start | bytes 38404
  13.4 1.0 copy-start.15
  13.4 7.9 %copy-start.17 = (bf16[64,64,128]{2,1,0:T(8,128)(2,1)S(1)}, bf16[64,64,128]{2,1,0:T(8,128)(2,1)}, u32[]{:S(2)}) copy-start(bf16[64,64,128]{2,1,0:T(8,128)(2,1)} %param.15) | copy-start | bytes 3145732
  14.4 9.4 %copy-start.18 = (bf16[3,64,128]{2,1,0:T(8,128)(2,1)S(1)}, bf16[3,64,128]{2,1,0:T(8,128)(2,1)}, u32[]{:S(2)}) copy-start(bf16[3,64,128]{2,1,0:T(8,128)(2,1)} %param.16) | copy-start | bytes 147460
  15.3 10.8 %collective-permute-start.3 = (bf16[18,64,128]{2,1,0:T(8,128)(2,1)}, bf16[18,64,128]{2,1,0:T(8,128)(2,1)}, u32[]{:S(2)}, u32[]{:S(2)}) collective-permute-start(bf16[18,64,128]{2,1,0:T(8,128)(2,1)} %get-tuple-element.36), channel_id=1, source_target_pairs={{0,4},{4,8},{8,12},{1,5},{5,9},{9,13},{2,6},{6,10},{10,14},{3,7},{... | collective-permute-start | bytes 884744 | tf_op jit(solution)/shard_map/ppermute | solution.py:27
  17.2 10.9 %collective-permute-start.4 = (bf16[18,64,128]{2,1,0:T(8,128)(2,1)}, bf16[18,64,128]{2,1,0:T(8,128)(2,1)}, u32[]{:S(2)}, u32[]{:S(2)}) collective-permute-start(bf16[18,64,128]{2,1,0:T(8,128)(2,1)} %get-tuple-element.35), channel_id=1, source_target_pairs={{4,0},{8,4},{12,8},{5,1},{9,5},{13,9},{6,2},{10,6},{14,10},{7,3},{... | collective-permute-start | bytes 884744 | tf_op jit(solution)/shard_map/ppermute | solution.py:29
  26.1 7.6 %copy-start.22 = (s32[16,128]{1,0:T(8,128)S(1)}, s32[16,128]{1,0:T(8,128)}, u32[]{:S(2)}) copy-start(s32[16,128]{1,0:T(8,128)} %param.20) | copy-start | bytes 24580
  26.1 89.3 %collective-permute-start.1 = (bf16[47,3,64]{0,2,1:T(8,128)(2,1)}, bf16[47,3,64]{0,2,1:T(8,128)(2,1)}, u32[]{:S(2)}, u32[]{:S(2)}) collective-permute-start(bf16[47,3,64]{0,2,1:T(8,128)(2,1)} %get-tuple-element.48), channel_id=1, source_target_pairs={{4,0},{8,4},{12,8},{5,1},{9,5},{13,9},{6,2},{10,6},{14,10},{7,3},{... | collective-permute-start | bytes 54152 | tf_op jit(solution)/shard_map/ppermute | solution.py:29
  31.8 36.8 %collective-permute-start.7 = (bf16[100,64,128]{2,1,0:T(8,128)(2,1)}, bf16[100,64,128]{2,1,0:T(8,128)(2,1)}, u32[]{:S(2)}, u32[]{:S(2)}) collective-permute-start(bf16[100,64,128]{2,1,0:T(8,128)(2,1)} %fusion.3.refs_0_), channel_id=1, source_target_pairs={{2,0},{0,2},{3,1},{1,3},{6,4},{4,6},{7,5},{5,7},{10,8},{8,10},{11,... | collective-permute-start | bytes 4915208 | tf_op jit(solution)/shard_map/ppermute | solution.py:39
  43.2 72.2 %collective-permute-start = (bf16[47,3,64]{0,2,1:T(8,128)(2,1)}, bf16[47,3,64]{0,2,1:T(8,128)(2,1)S(1)}, u32[]{:S(2)}, u32[]{:S(2)}) collective-permute-start(bf16[47,3,64]{0,2,1:T(8,128)(2,1)} %get-tuple-element.47), channel_id=1, source_target_pairs={{0,4},{4,8},{8,12},{1,5},{5,9},{9,13},{2,6},{6,10},{10,14},{3,7},{... | collective-permute-start | bytes 54152 | tf_op jit(solution)/shard_map/ppermute | solution.py:27
  46.6 6.8 %collective-permute-start.5 = (bf16[18,3,256]{2,1,0:T(4,128)(2,1)S(1)}, bf16[18,3,256]{2,1,0:T(4,128)(2,1)S(1)}, u32[]{:S(2)}, u32[]{:S(2)}) collective-permute-start(bf16[18,3,256]{2,1,0:T(4,128)(2,1)S(1)} %get-tuple-element.46), channel_id=1, source_target_pairs={{0,4},{4,8},{8,12},{1,5},{5,9},{9,13},{2,6},{6,10},{10,14},{3,7},{... | collective-permute-start | bytes 82952 | tf_op jit(solution)/shard_map/ppermute | solution.py:27
  49.2 5.1 %collective-permute-start.6 = (bf16[18,3,256]{2,1,0:T(4,128)(2,1)S(1)}, bf16[18,3,256]{2,1,0:T(4,128)(2,1)S(1)}, u32[]{:S(2)}, u32[]{:S(2)}) collective-permute-start(bf16[18,3,256]{2,1,0:T(4,128)(2,1)S(1)} %get-tuple-element.45), channel_id=1, source_target_pairs={{4,0},{8,4},{12,8},{5,1},{9,5},{13,9},{6,2},{10,6},{14,10},{7,3},{... | collective-permute-start | bytes 82952 | tf_op jit(solution)/shard_map/ppermute | solution.py:29
  55.7 12.9 %copy-start.7 = (s32[924]{0:T(1024)S(1)}, s32[924]{0:T(1024)}, u32[]{:S(2)}) copy-start(s32[924]{0:T(1024)} %concatenate.47.codes_ref) | copy-start | bytes 11092
  55.7 12.9 %copy-start.10 = (s32[32]{0:T(128)S(1)}, s32[32]{0:T(128)}, u32[]{:S(2)}) copy-start(s32[32]{0:T(128)} %get-tuple-element.19.groups_ref) | copy-start | bytes 388
  55.7 12.9 %copy-start.11 = (bf16[26,16,256]{2,1,0:T(8,128)(2,1)S(1)}, bf16[26,16,256]{2,1,0:T(8,128)(2,1)}, u32[]{:S(2)}) copy-start(bf16[26,16,256]{2,1,0:T(8,128)(2,1)} %constant.133.clone.factor_ref) | copy-start | bytes 638980
  55.7 12.9 %copy-start.13 = (bf16[26,16,256]{2,1,0:T(8,128)(2,1)S(1)}, bf16[26,16,256]{2,1,0:T(8,128)(2,1)}, u32[]{:S(2)}) copy-start(bf16[26,16,256]{2,1,0:T(8,128)(2,1)} %constant.134.clone.added_ref) | copy-start | bytes 638980
  58.3 49.8 %collective-permute-start.8 = (bf16[64,64,64]{2,1,0:T(8,128)(2,1)S(1)}, bf16[64,64,64]{2,1,0:T(8,128)(2,1)S(1)}, u32[]{:S(2)}, u32[]{:S(2)}) collective-permute-start(bf16[64,64,64]{2,1,0:T(8,128)(2,1)S(1)} %get-tuple-element.53), channel_id=1, source_target_pairs={{2,0},{0,2},{3,1},{1,3},{6,4},{4,6},{7,5},{5,7},{10,8},{8,10},{11,... | collective-permute-start | bytes 1572872 | tf_op jit(solution)/shard_map/ppermute | solution.py:39
  109.5 5.9 %copy-start.19 = (bf16[3,64,128]{2,1,0:T(8,128)(2,1)S(1)}, bf16[3,64,128]{2,1,0:T(8,128)(2,1)}, u32[]{:S(2)}) copy-start(bf16[3,64,128]{2,1,0:T(8,128)(2,1)} %param.16) | copy-start | bytes 147460
  109.5 15.7 %collective-permute-start.9 = (bf16[64,64,64]{2,1,0:T(8,128)(2,1)}, bf16[64,64,64]{2,1,0:T(8,128)(2,1)}, u32[]{:S(2)}, u32[]{:S(2)}) collective-permute-start(bf16[64,64,64]{2,1,0:T(8,128)(2,1)} %add_convert_fusion), channel_id=1, source_target_pairs={{1,0},{0,1},{3,2},{2,3},{5,4},{4,5},{7,6},{6,7},{9,8},{8,9},{11,10... | collective-permute-start | bytes 1572872 | tf_op jit(solution)/shard_map/ppermute | solution.py:39
  115.4 4.3 %collective-permute-start.10 = (bf16[8,64,64]{2,1,0:T(8,128)(2,1)}, bf16[8,64,64]{2,1,0:T(8,128)(2,1)}, u32[]{:S(2)}, u32[]{:S(2)}) collective-permute-start(bf16[8,64,64]{2,1,0:T(8,128)(2,1)} %convolution_convert_fusion), channel_id=1, source_target_pairs={{1,0},{0,1},{3,2},{2,3},{5,4},{4,5},{7,6},{6,7},{9,8},{8,9},{11,10... | collective-permute-start | bytes 196616 | tf_op jit(solution)/shard_map/ppermute | solution.py:39
  120.7 49.7 %collective-permute-start.11 = (bf16[16,64,64]{2,1,0:T(8,128)(2,1)S(1)}, bf16[16,64,64]{2,1,0:T(8,128)(2,1)S(1)}, u32[]{:S(2)}, u32[]{:S(2)}) collective-permute-start(bf16[16,64,64]{2,1,0:T(8,128)(2,1)S(1)} %pad_maximum_fusion.4), channel_id=1, source_target_pairs={{4,0},{8,4},{12,8},{0,12},{5,1},{9,5},{13,9},{1,13},{6,2},{10,6},{... | collective-permute-start | bytes 393224 | tf_op jit(solution)/shard_map/ppermute | solution.py:39
  120.8 49.7 %collective-permute-start.12 = (bf16[16,64,64]{2,1,0:T(8,128)(2,1)S(1)}, bf16[16,64,64]{2,1,0:T(8,128)(2,1)S(1)}, u32[]{:S(2)}, u32[]{:S(2)}) collective-permute-start(bf16[16,64,64]{2,1,0:T(8,128)(2,1)S(1)} %pad_maximum_fusion.4), channel_id=1, source_target_pairs={{8,0},{12,4},{0,8},{4,12},{9,1},{13,5},{1,9},{5,13},{10,2},{14,6},... | collective-permute-start | bytes 393224 | tf_op jit(solution)/shard_map/ppermute | solution.py:39
  122.9 47.5 %collective-permute-start.13 = (bf16[16,64,64]{2,1,0:T(8,128)(2,1)S(1)}, bf16[16,64,64]{2,1,0:T(8,128)(2,1)S(1)}, u32[]{:S(2)}, u32[]{:S(2)}) collective-permute-start(bf16[16,64,64]{2,1,0:T(8,128)(2,1)S(1)} %pad_maximum_fusion.4), channel_id=1, source_target_pairs={{12,0},{0,4},{4,8},{8,12},{13,1},{1,5},{5,9},{9,13},{14,2},{2,6},{... | collective-permute-start | bytes 393224 | tf_op jit(solution)/shard_map/ppermute | solution.py:39
  127.0 5.9 %copy-start.4 = (f32[32,3,128]{2,1,0:T(4,128)S(1)}, f32[32,3,128]{2,1,0:T(4,128)}, u32[]{:S(2)}) copy-start(f32[32,3,128]{2,1,0:T(4,128)} %get-tuple-element.41.own_ref) | copy-start | bytes 147460
  127.0 5.9 %copy-start.6 = (s32[924]{0:T(1024)S(1)}, s32[924]{0:T(1024)}, u32[]{:S(2)}) copy-start(s32[924]{0:T(1024)} %concatenate.44.codes_ref) | copy-start | bytes 11092
  127.0 5.9 %copy-start.9 = (s32[32]{0:T(128)S(1)}, s32[32]{0:T(128)}, u32[]{:S(2)}) copy-start(s32[32]{0:T(128)} %get-tuple-element.21.groups_ref) | copy-start | bytes 388
  127.0 5.9 %copy-start.12 = (bf16[26,16,256]{2,1,0:T(8,128)(2,1)S(1)}, bf16[26,16,256]{2,1,0:T(8,128)(2,1)}, u32[]{:S(2)}) copy-start(bf16[26,16,256]{2,1,0:T(8,128)(2,1)} %constant.133.clone.factor_ref) | copy-start | bytes 638980
  127.0 5.9 %copy-start.14 = (bf16[26,16,256]{2,1,0:T(8,128)(2,1)S(1)}, bf16[26,16,256]{2,1,0:T(8,128)(2,1)}, u32[]{:S(2)}) copy-start(bf16[26,16,256]{2,1,0:T(8,128)(2,1)} %constant.134.clone.added_ref) | copy-start | bytes 638980
  127.5 43.0 %collective-permute-start.14 = (bf16[47,64,64]{2,1,0:T(8,128)(2,1)S(1)}, bf16[47,64,64]{2,1,0:T(8,128)(2,1)S(1)}, u32[]{:S(2)}, u32[]{:S(2)}) collective-permute-start(bf16[47,64,64]{2,1,0:T(8,128)(2,1)S(1)} %slice.80), channel_id=1, source_target_pairs={{0,4},{4,8},{8,12},{1,5},{5,9},{9,13},{2,6},{6,10},{10,14},{3,7},{... | collective-permute-start | bytes 1155080 | tf_op jit(solution)/shard_map/ppermute | solution.py:27
  129.4 41.1 %collective-permute-start.15 = (bf16[47,64,64]{2,1,0:T(8,128)(2,1)S(1)}, bf16[47,64,64]{2,1,0:T(8,128)(2,1)S(1)}, u32[]{:S(2)}, u32[]{:S(2)}) collective-permute-start(bf16[47,64,64]{2,1,0:T(8,128)(2,1)S(1)} %slice.81), channel_id=1, source_target_pairs={{4,0},{8,4},{12,8},{5,1},{9,5},{13,9},{6,2},{10,6},{14,10},{7,3},{... | collective-permute-start | bytes 1155080 | tf_op jit(solution)/shard_map/ppermute | solution.py:29
  170.5 3.3 %copy-start.3 = (f32[64,3,64]{2,1,0:T(4,128)S(1)}, f32[64,3,64]{2,1,0:T(4,128)}, u32[]{:S(2)}) copy-start(f32[64,3,64]{2,1,0:T(4,128)} %maximum_convert_fusion.parent_skeleton_ref) | copy-start | bytes 147460
  173.5 1.6 copy-start.1
  173.5 1.6 copy-start.5
  173.5 1.6 copy-start.8
  205.2 1.0 copy-start.2
  206.2 4.4 %collective-permute-start.19 = (bf16[64,32,128]{2,1,0:T(8,128)(2,1)S(1)}, bf16[64,32,128]{2,1,0:T(8,128)(2,1)S(1)}, u32[]{:S(2)}, u32[]{:S(2)}) collective-permute-start(bf16[64,32,128]{2,1,0:T(8,128)(2,1)S(1)} %constant_dynamic-slice_fusion), channel_id=1, source_target_pairs={{1,0},{0,1},{3,2},{2,3},{5,4},{4,5},{7,6},{6,7},{9,8},{8,9},{11,10... | collective-permute-start | bytes 1572872 | tf_op jit(solution)/shard_map/ppermute | solution.py:39

commit v3 on v2

--- a/solution.py
+++ b/solution.py
@@ -316,9 +316,15 @@
     near_parts = lax.axis_size("near")
     window = own + 2 * near_reach
 
-    wide = paired(jnp.transpose(charges, (2, 1, 0)), rhs_index, 1)
-    wide = mine(padded(wide, "leaf", near_reach), 0, window)
-    shares = [wide] + [rotated(wide, "near", k) for k in range(1, near_parts)]
+    cells = jnp.transpose(charges, (2, 1, 0))
+
+    def around(share):
+        both = paired(share, rhs_index, 1)
+        return mine(padded(both, "leaf", near_reach), 0, window)
+
+    others = [rotated(cells, "near", k) for k in range(1, near_parts)]
+    wide = around(cells)
+    shares = [wide] + [around(share) for share in others]
 
     point_cells = jnp.transpose(points, (2, 0, 1))
     border_points = mine(padded(point_cells, "leaf", near_reach), 0, window)

time: 217 us -> 212 us (0.977)
    ppermute x12 -> x13, waiting for transfers between devices: 11.5 us -> 1.57 us  [rotated(): lax.ppermute(cells, axis, [((i + step) % count, i) for i in range(count)])]
    ppermute x4 -> x5, waiting for transfers between devices: 1.59 us -> 7.25 us  [halo(): lax.ppermute(tail, axis, [(i, i + 1) for i in range(ends)])]
    ppermute x12 -> x13, starting transfers between devices: 17.8 us -> 14.7 us  [rotated(): lax.ppermute(cells, axis, [((i + step) % count, i) for i in range(count)])]
    ppermute x4 -> x5, waiting for transfers between devices: 0.93 us -> 3.75 us  [halo(): lax.ppermute(head, axis, [(i + 1, i) for i in range(ends)])]
    ppermute x4 -> x5, starting transfers between devices: 9.76 us -> 12.2 us  [halo(): lax.ppermute(tail, axis, [(i, i + 1) for i in range(ends)])]
    ppermute x4 -> x5, starting transfers between devices: 12.2 us -> 14.6 us  [halo(): lax.ppermute(head, axis, [(i + 1, i) for i in range(ends)])]
    select_n x3 -> x4, other arithmetic: 4.35 us -> 6.31 us  [paired(): jnp.where(first, cells, other)]
    unnamed x54 -> x64, local copies, waits for them, and re-layouts: 16.5 us -> 14.7 us
  transfers between devices with their start and end apart: 20 -> 23, of which waited for: 4 -> 5; matrix products, arithmetic and copies ran while one was open for 19% -> 17% of each run, Pallas kernels for 36% -> 36%
where the time goes in v3:
time: 212 us; the launch traced here: 210 us
  Pallas kernels  106 us (50%)
  starting transfers between devices  41.4 us (20%)
  local copies, waits for them, and re-layouts  25.1 us (12%)
  other arithmetic  21 us (10%)
  waiting for transfers between devices  12.6 us (6%)
  matrix products  3.07 us (1%)
    pallas_call x2, Pallas kernels, near_call(): pl.pallas_call(functools.partial(near_kernel, slots, near_parts, first, s...  76 us
    pallas_call x1, Pallas kernels, per_device(): pl.pallas_call(functools.partial(far_kernel, leaf_far.shape[0], parent_fa...  30 us
    unnamed x64, local copies, waits for them, and re-layouts  14.7 us
    ppermute x13, starting transfers between devices, rotated(): lax.ppermute(cells, axis, [((i + step) % count, i) for i in range(count)])  14.7 us
    ppermute x5, starting transfers between devices, halo(): lax.ppermute(head, axis, [(i + 1, i) for i in range(ends)])  14.6 us
    ppermute x5, starting transfers between devices, halo(): lax.ppermute(tail, axis, [(i, i + 1) for i in range(ends)])  12.2 us
    ppermute x5, waiting for transfers between devices, halo(): lax.ppermute(tail, axis, [(i, i + 1) for i in range(ends)])  7.25 us
    select_n x4, other arithmetic, paired(): jnp.where(first, cells, other)  6.31 us
  transfers between devices with their start and end apart: 23, of which 5 were waited for; matrix products, arithmetic and copies ran while one was open for 17% of the time, Pallas kernels for 36%

profile of v3, /device:TPU:13, one launch (start us, length us, event | category | flops | bytes accessed | tf_op | source)
XLA Modules:
  0.0 209.8 jit_solution(8613640104351802614)
XLA Ops:
  0.0 3.3 %copy.43 = bf16[128,32,128]{0,1,2:T(8,128)(2,1)} copy(bf16[128,32,128]{2,1,0:T(8,128)(2,1)} %param.13) | data formatting | bytes 2097152 | tf_op args[1]
  4.0 1.2 collective-permute-start.7
  5.2 1.3 collective-permute-start.21
  6.6 1.1 collective-permute-start.20
  7.7 1.4 collective-permute-start.19
  9.9 2.0 constant_dynamic-slice_fusion.2
  12.1 1.5 constant_dynamic-slice_fusion.1
  16.3 4.4 %copy.56 = bf16[128,64,64]{1,0,2:T(8,128)(2,1)} copy(bf16[128,64,64]{2,1,0:T(8,128)(2,1)} %constant_dynamic-slice_fusion.2) | data formatting | bytes 2097152
  20.9 2.6 %copy.57 = bf16[64,64,64]{1,0,2:T(8,128)(2,1)S(1)} copy(bf16[64,64,64]{2,1,0:T(8,128)(2,1)} %constant_dynamic-slice_fusion.1) | data formatting | bytes 1048576
  24.7 3.0 %collective-permute-start.1 = (bf16[47,3,64]{0,2,1:T(8,128)(2,1)}, bf16[47,3,64]{0,2,1:T(8,128)(2,1)S(1)}, u32[]{:S(2)}, u32[]{:S(2)}) collective-permute-start(bf16[47,3,64]{0,2,1:T(8,128)(2,1)} %get-tuple-element.52), channel_id=1, source_target_pairs={{4,0},{8,4},{12,8},{5,1},{9,5},{13,9},{6,2},{10,6},{14,10},{7,3},{... | collective-permute-start | bytes 54152 | tf_op jit(solution)/shard_map/ppermute | solution.py:29
  27.7 2.3 %collective-permute-start.5 = (bf16[18,3,256]{2,1,0:T(4,128)(2,1)S(1)}, bf16[18,3,256]{2,1,0:T(4,128)(2,1)S(1)}, u32[]{:S(2)}, u32[]{:S(2)}) collective-permute-start(bf16[18,3,256]{2,1,0:T(4,128)(2,1)S(1)} %get-tuple-element.50), channel_id=1, source_target_pairs={{0,4},{4,8},{8,12},{1,5},{5,9},{9,13},{2,6},{6,10},{10,14},{3,7},{... | collective-permute-start | bytes 82952 | tf_op jit(solution)/shard_map/ppermute | solution.py:27
  30.0 3.0 %collective-permute-start.6 = (bf16[18,3,256]{2,1,0:T(4,128)(2,1)S(1)}, bf16[18,3,256]{2,1,0:T(4,128)(2,1)S(1)}, u32[]{:S(2)}, u32[]{:S(2)}) collective-permute-start(bf16[18,3,256]{2,1,0:T(4,128)(2,1)S(1)} %get-tuple-element.49), channel_id=1, source_target_pairs={{4,0},{8,4},{12,8},{5,1},{9,5},{13,9},{6,2},{10,6},{14,10},{7,3},{... | collective-permute-start | bytes 82952 | tf_op jit(solution)/shard_map/ppermute | solution.py:29
  33.7 2.3 %collective-permute-start = (bf16[47,3,64]{0,2,1:T(8,128)(2,1)}, bf16[47,3,64]{0,2,1:T(8,128)(2,1)S(1)}, u32[]{:S(2)}, u32[]{:S(2)}) collective-permute-start(bf16[47,3,64]{0,2,1:T(8,128)(2,1)} %get-tuple-element.51), channel_id=1, source_target_pairs={{0,4},{4,8},{8,12},{1,5},{5,9},{9,13},{2,6},{6,10},{10,14},{3,7},{... | collective-permute-start | bytes 54152 | tf_op jit(solution)/shard_map/ppermute | solution.py:27
  36.0 2.3 %collective-permute-start.8 = (bf16[128,32,128]{2,1,0:T(8,128)(2,1)}, bf16[128,32,128]{2,1,0:T(8,128)(2,1)S(1)}, u32[]{:S(2)}, u32[]{:S(2)}) collective-permute-start(bf16[128,32,128]{2,1,0:T(8,128)(2,1)} %collective-permute-done.7), channel_id=1, source_target_pairs={{1,0},{0,1},{3,2},{2,3},{5,4},{4,5},{7,6},{6,7},{9,8},{8,9},{11,10... | collective-permute-start | bytes 3145736 | tf_op jit(solution)/shard_map/ppermute | solution.py:39
  38.9 1.7 broadcast_select_fusion.3
  40.6 1.9 collective-permute-start.3
  42.5 3.4 %collective-permute-start.4 = (bf16[18,64,128]{2,1,0:T(8,128)(2,1)S(1)}, bf16[18,64,128]{2,1,0:T(8,128)(2,1)S(1)}, u32[]{:S(2)}, u32[]{:S(2)}) collective-permute-start(bf16[18,64,128]{2,1,0:T(8,128)(2,1)S(1)} %get-tuple-element.39), channel_id=1, source_target_pairs={{4,0},{8,4},{12,8},{5,1},{9,5},{13,9},{6,2},{10,6},{14,10},{7,3},{... | collective-permute-start | bytes 884744 | tf_op jit(solution)/shard_map/ppermute | solution.py:29
  46.8 4.3 %collective-permute-done.3 = bf16[18,64,128]{2,1,0:T(8,128)(2,1)S(1)} collective-permute-done((bf16[18,64,128]{2,1,0:T(8,128)(2,1)S(1)}, bf16[18,64,128]{2,1,0:T(8,128)(2,1)S(1)}, u32[]{:S(2)}, u32[]{:S(2)}) %collective-permute-start.3) | collective-permute-done | bytes 294944 | tf_op jit(solution)/shard_map/ppermute | solution.py:27
  51.1 1.7 collective-permute-done.4
  52.8 2.0 fusion.6.refs_0_
  54.9 2.0 broadcast_select_fusion.1
  56.9 2.2 %collective-permute-start.9 = (bf16[18,64,128]{2,1,0:T(8,128)(2,1)S(1)}, bf16[18,64,128]{2,1,0:T(8,128)(2,1)S(1)}, u32[]{:S(2)}, u32[]{:S(2)}) collective-permute-start(bf16[18,64,128]{2,1,0:T(8,128)(2,1)S(1)} %get-tuple-element.36), channel_id=1, source_target_pairs={{0,4},{4,8},{8,12},{1,5},{5,9},{9,13},{2,6},{6,10},{10,14},{3,7},{... | collective-permute-start | bytes 884744 | tf_op jit(solution)/shard_map/ppermute | solution.py:27
  59.1 3.2 %collective-permute-start.10 = (bf16[18,64,128]{2,1,0:T(8,128)(2,1)S(1)}, bf16[18,64,128]{2,1,0:T(8,128)(2,1)S(1)}, u32[]{:S(2)}, u32[]{:S(2)}) collective-permute-start(bf16[18,64,128]{2,1,0:T(8,128)(2,1)S(1)} %get-tuple-element.35), channel_id=1, source_target_pairs={{4,0},{8,4},{12,8},{5,1},{9,5},{13,9},{6,2},{10,6},{14,10},{7,3},{... | collective-permute-start | bytes 884744 | tf_op jit(solution)/shard_map/ppermute | solution.py:29
  63.5 2.9 %collective-permute-done.9 = bf16[18,64,128]{2,1,0:T(8,128)(2,1)S(1)} collective-permute-done((bf16[18,64,128]{2,1,0:T(8,128)(2,1)S(1)}, bf16[18,64,128]{2,1,0:T(8,128)(2,1)S(1)}, u32[]{:S(2)}, u32[]{:S(2)}) %collective-permute-start.9) | collective-permute-done | bytes 294944 | tf_op jit(solution)/shard_map/ppermute | solution.py:27
  66.4 2.0 collective-permute-done.10
  68.4 2.0 fusion.3.refs_1_
  70.6 38.3 %near_field.2.refs_0_ = f32[32,128,64]{2,1,0:T(8,128)} custom-call(s32[924]{0:T(1024)S(1)} %copy-done.12, s32[32]{0:T(128)S(1)} %copy-done.15, f32[32,3,128]{2,1,0:T(4,128)S(1)} %get-tuple-element.46.own_ref, f32[100,3,256]{2,1,0:T(4,128)S(1)} %fusion.13.border_ref, bf16[26,16,256]{2,1,0:T(8,128)(2,1)S(1)} %copy-done.16, ...), custom_call_target="tpu_custom_call" | custom-call | flops 30000001024 | bytes 16000000 | tf_op jit(solution)/shard_map/near_field/pallas_call | solution.py:363
  108.9 1.3 add_convert_fusion
  110.2 1.6 collective-permute-start.12
  111.7 2.3 %convolution_convert_fusion = bf16[8,64,64]{2,1,0:T(8,128)(2,1)} fusion(bf16[8,512,64]{2,1,0:T(8,128)(2,1)S(1)} %bitcast.29, bf16[8,512,64]{2,1,0:T(8,128)(2,1)} %bitcast.10), kind=kOutput, calls=%fused_computation.21 | convolution fusion | flops 33587200 | bytes 1114112 | tf_op jit(solution)/shard_map/pkb,pkc->pbc/dot_general | solution.py:396
  114.1 0.8 dynamic-slice_maximum_fusion
  114.9 1.7 copy.55
  116.7 1.0 convert_element_type.21.leaf_skeleton_ref
  117.6 1.0 broadcast_select_fusion.9
  118.7 1.4 collective-permute-start.14
  120.1 1.3 collective-permute-start.16
  121.3 1.7 broadcast_select_fusion.5
  123.6 3.4 %collective-permute-start.17 = (bf16[47,64,64]{2,1,0:T(8,128)(2,1)S(1)}, bf16[47,64,64]{2,1,0:T(8,128)(2,1)S(1)}, u32[]{:S(2)}, u32[]{:S(2)}) collective-permute-start(bf16[47,64,64]{2,1,0:T(8,128)(2,1)S(1)} %slice.88), channel_id=1, source_target_pairs={{0,4},{4,8},{8,12},{1,5},{5,9},{9,13},{2,6},{6,10},{10,14},{3,7},{... | collective-permute-start | bytes 1155080 | tf_op jit(solution)/shard_map/ppermute | solution.py:27
  127.1 2.0 collective-permute-start.18
  129.2 37.7 %near_field.3.refs_1_ = f32[32,128,64]{2,1,0:T(8,128)} custom-call(s32[924]{0:T(1024)S(1)} %copy-done.11, s32[32]{0:T(128)S(1)} %copy-done.14, f32[32,3,128]{2,1,0:T(4,128)S(1)} %copy-done.9, f32[100,3,256]{2,1,0:T(4,128)S(1)} %fusion.13.border_ref, bf16[26,16,256]{2,1,0:T(8,128)(2,1)S(1)} %copy-done.17, bf16[26,16,256]{2,1,0:T(8,128)(2,1)S(1)} %copy-done.19, ...), custom_call_target="tpu_custom_call" | custom-call | flops 30000001024 | bytes 16000000 | tf_op jit(solution)/shard_map/near_field/pallas_call | solution.py:363
  166.9 3.0 %fusion.1.leaf_moments_ref = bf16[158,64,64]{2,1,0:T(8,128)(2,1)} fusion(s32[]{:T(128)S(6)} %select_n.149, bf16[47,64,64]{2,1,0:T(8,128)(2,1)S(1)} %collective-permute-done.17, bf16[128,64,64]{2,1,0:T(8,128)(2,1)S(1)} %pad_maximum_fusion, bf16[47,64,64]{2,1,0:T(8,128)(2,1)S(1)} %collective-permute-done.18), kind=kLoop, calls=%fused_computation.12 | loop fusion | flops 1294336 | bytes 3112964 | tf_op jit(solution)/shard_map/concatenate | solution.py:412
  170.2 1.3 copy-done.2
  171.5 30.0 %far_field.1 = bf16[64,64,128]{2,1,0:T(8,128)(2,1)S(1)} custom-call(s32[1024]{0:T(1024)S(1)} %copy-done.10, s32[128]{0:T(128)S(1)} %copy-done.13, s32[1]{0:T(128)} %bitcast.2.own_start_ref, f32[158,3,64]{2,1,0:T(4,128)S(1)} %convert_element_type.21.leaf_skeleton_ref, bf16[158,64,64]{2,1,0:T(8,128)(2,1)} %fusion.1.leaf_moments_ref, ...), custom_call_target="tpu_custom_call" | custom-call | tf_op jit(solution)/shard_map/far_field/pallas_call | solution.py:424
  201.6 1.0 copy-done.5
  202.6 2.1 collective-permute-start.22
  204.7 1.5 collective-permute-done.22
  206.2 1.3 broadcast_select_fusion.7
  207.6 2.3 %copy.51 = bf16[128,32,128]{2,1,0:T(8,128)(2,1)} copy(bf16[128,32,128]{0,1,2:T(8,128)(2,1)S(1)} %maximum_bitcast_fusion) | data formatting | bytes 2097152 | tf_op jit(solution)/shard_map/transpose | solution.py:459
  (115 shorter events, 10.1 us)
Async XLA Ops:
  0.0 9.9 %copy-start = (bf16[128,64,128]{2,1,0:T(8,128)(2,1)S(1)}, bf16[128,64,128]{2,1,0:T(8,128)(2,1)}, u32[]{:S(2)}) copy-start(bf16[128,64,128]{2,1,0:T(8,128)(2,1)} %param.14) | copy-start | bytes 6291460
  0.0 5.2 %copy-start.25 = (bf16[3,64,16]{1,2,0:T(8,128)(2,1)S(1)}, bf16[3,64,16]{1,2,0:T(8,128)(2,1)}, u32[]{:S(2)}) copy-start(bf16[3,64,16]{1,2,0:T(8,128)(2,1)} %param.17) | copy-start | bytes 18436
  0.0 9.1 %copy-start.26 = (s32[16,16]{1,0:T(8,128)S(1)}, s32[16,16]{1,0:T(8,128)}, u32[]{:S(2)}) copy-start(s32[16,16]{1,0:T(8,128)} %param.21) | copy-start | bytes 3076
  0.0 9.8 %copy-start.28 = (s32[128]{0:T(128)S(1)}, s32[128]{0:T(128)}, u32[]{:S(2)}) copy-start(s32[128]{0:T(128)} %param.19) | copy-start | bytes 1540
  3.3 35.5 %collective-permute-start.2 = (bf16[128,32,128]{2,1,0:T(8,128)(2,1)}, bf16[128,32,128]{2,1,0:T(8,128)(2,1)}, u32[]{:S(2)}, u32[]{:S(2)}) collective-permute-start(bf16[128,32,128]{2,1,0:T(8,128)(2,1)} %bitcast.6), channel_id=1, source_target_pairs={{1,0},{0,1},{3,2},{2,3},{5,4},{4,5},{7,6},{6,7},{9,8},{8,9},{11,10... | collective-permute-start | bytes 3145736 | tf_op jit(solution)/shard_map/ppermute | solution.py:39
  4.0 32.0 %collective-permute-start.7 = (bf16[128,32,128]{2,1,0:T(8,128)(2,1)}, bf16[128,32,128]{2,1,0:T(8,128)(2,1)}, u32[]{:S(2)}, u32[]{:S(2)}) collective-permute-start(bf16[128,32,128]{2,1,0:T(8,128)(2,1)} %bitcast.6), channel_id=1, source_target_pairs={{2,0},{0,2},{3,1},{1,3},{6,4},{4,6},{7,5},{5,7},{10,8},{8,10},{11,... | collective-permute-start | bytes 3145736 | tf_op jit(solution)/shard_map/ppermute | solution.py:39
  5.2 19.4 %collective-permute-start.21 = (bf16[16,3,64]{2,1,0:T(4,128)(2,1)S(1)}, bf16[16,3,64]{2,1,0:T(4,128)(2,1)S(1)}, u32[]{:S(2)}, u32[]{:S(2)}) collective-permute-start(bf16[16,3,64]{2,1,0:T(4,128)(2,1)S(1)} %bitcast.35), channel_id=1, source_target_pairs={{12,0},{0,4},{4,8},{8,12},{13,1},{1,5},{5,9},{9,13},{14,2},{2,6},{... | collective-permute-start | bytes 18440 | tf_op jit(solution)/shard_map/ppermute | solution.py:39
  6.6 21.1 %collective-permute-start.20 = (bf16[16,3,64]{2,1,0:T(4,128)(2,1)S(1)}, bf16[16,3,64]{2,1,0:T(4,128)(2,1)S(1)}, u32[]{:S(2)}, u32[]{:S(2)}) collective-permute-start(bf16[16,3,64]{2,1,0:T(4,128)(2,1)S(1)} %bitcast.36), channel_id=1, source_target_pairs={{8,0},{12,4},{0,8},{4,12},{9,1},{13,5},{1,9},{5,13},{10,2},{14,6},... | collective-permute-start | bytes 18440 | tf_op jit(solution)/shard_map/ppermute | solution.py:39
  7.7 22.3 %collective-permute-start.19 = (bf16[16,3,64]{2,1,0:T(4,128)(2,1)S(1)}, bf16[16,3,64]{2,1,0:T(4,128)(2,1)S(1)}, u32[]{:S(2)}, u32[]{:S(2)}) collective-permute-start(bf16[16,3,64]{2,1,0:T(4,128)(2,1)S(1)} %bitcast.37), channel_id=1, source_target_pairs={{4,0},{8,4},{12,8},{0,12},{5,1},{9,5},{13,9},{1,13},{6,2},{10,6},{... | collective-permute-start | bytes 18440 | tf_op jit(solution)/shard_map/ppermute | solution.py:39
  9.9 2.1 copy-start.24
  9.9 2.2 %copy-start.20 = (bf16[64,64,128]{2,1,0:T(8,128)(2,1)S(1)}, bf16[64,64,128]{2,1,0:T(8,128)(2,1)}, u32[]{:S(2)}) copy-start(bf16[64,64,128]{2,1,0:T(8,128)(2,1)} %param.15) | copy-start | bytes 3145732
  12.0 1.7 copy-start.23
  12.0 2.6 %copy-start.21 = (bf16[3,64,128]{2,1,0:T(8,128)(2,1)S(1)}, bf16[3,64,128]{2,1,0:T(8,128)(2,1)}, u32[]{:S(2)}) copy-start(bf16[3,64,128]{2,1,0:T(8,128)(2,1)} %param.16) | copy-start | bytes 147460
  12.0 3.3 %copy-start.27 = (s32[16,128]{1,0:T(8,128)S(1)}, s32[16,128]{1,0:T(8,128)}, u32[]{:S(2)}) copy-start(s32[16,128]{1,0:T(8,128)} %param.20) | copy-start | bytes 24580
  24.7 89.4 %collective-permute-start.1 = (bf16[47,3,64]{0,2,1:T(8,128)(2,1)}, bf16[47,3,64]{0,2,1:T(8,128)(2,1)S(1)}, u32[]{:S(2)}, u32[]{:S(2)}) collective-permute-start(bf16[47,3,64]{0,2,1:T(8,128)(2,1)} %get-tuple-element.52), channel_id=1, source_target_pairs={{4,0},{8,4},{12,8},{5,1},{9,5},{13,9},{6,2},{10,6},{14,10},{7,3},{... | collective-permute-start | bytes 54152 | tf_op jit(solution)/shard_map/ppermute | solution.py:29
  27.7 6.0 %collective-permute-start.5 = (bf16[18,3,256]{2,1,0:T(4,128)(2,1)S(1)}, bf16[18,3,256]{2,1,0:T(4,128)(2,1)S(1)}, u32[]{:S(2)}, u32[]{:S(2)}) collective-permute-start(bf16[18,3,256]{2,1,0:T(4,128)(2,1)S(1)} %get-tuple-element.50), channel_id=1, source_target_pairs={{0,4},{4,8},{8,12},{1,5},{5,9},{9,13},{2,6},{6,10},{10,14},{3,7},{... | collective-permute-start | bytes 82952 | tf_op jit(solution)/shard_map/ppermute | solution.py:27
  30.0 8.3 %collective-permute-start.6 = (bf16[18,3,256]{2,1,0:T(4,128)(2,1)S(1)}, bf16[18,3,256]{2,1,0:T(4,128)(2,1)S(1)}, u32[]{:S(2)}, u32[]{:S(2)}) collective-permute-start(bf16[18,3,256]{2,1,0:T(4,128)(2,1)S(1)} %get-tuple-element.49), channel_id=1, source_target_pairs={{4,0},{8,4},{12,8},{5,1},{9,5},{13,9},{6,2},{10,6},{14,10},{7,3},{... | collective-permute-start | bytes 82952 | tf_op jit(solution)/shard_map/ppermute | solution.py:29
  33.7 80.4 %collective-permute-start = (bf16[47,3,64]{0,2,1:T(8,128)(2,1)}, bf16[47,3,64]{0,2,1:T(8,128)(2,1)S(1)}, u32[]{:S(2)}, u32[]{:S(2)}) collective-permute-start(bf16[47,3,64]{0,2,1:T(8,128)(2,1)} %get-tuple-element.51), channel_id=1, source_target_pairs={{0,4},{4,8},{8,12},{1,5},{5,9},{9,13},{2,6},{6,10},{10,14},{3,7},{... | collective-permute-start | bytes 54152 | tf_op jit(solution)/shard_map/ppermute | solution.py:27
  36.0 18.9 %collective-permute-start.8 = (bf16[128,32,128]{2,1,0:T(8,128)(2,1)}, bf16[128,32,128]{2,1,0:T(8,128)(2,1)S(1)}, u32[]{:S(2)}, u32[]{:S(2)}) collective-permute-start(bf16[128,32,128]{2,1,0:T(8,128)(2,1)} %collective-permute-done.7), channel_id=1, source_target_pairs={{1,0},{0,1},{3,2},{2,3},{5,4},{4,5},{7,6},{6,7},{9,8},{8,9},{11,10... | collective-permute-start | bytes 3145736 | tf_op jit(solution)/shard_map/ppermute | solution.py:39
  40.6 10.5 %collective-permute-start.3 = (bf16[18,64,128]{2,1,0:T(8,128)(2,1)S(1)}, bf16[18,64,128]{2,1,0:T(8,128)(2,1)S(1)}, u32[]{:S(2)}, u32[]{:S(2)}) collective-permute-start(bf16[18,64,128]{2,1,0:T(8,128)(2,1)S(1)} %get-tuple-element.40), channel_id=1, source_target_pairs={{0,4},{4,8},{8,12},{1,5},{5,9},{9,13},{2,6},{6,10},{10,14},{3,7},{... | collective-permute-start | bytes 884744 | tf_op jit(solution)/shard_map/ppermute | solution.py:27
  42.5 10.3 %collective-permute-start.4 = (bf16[18,64,128]{2,1,0:T(8,128)(2,1)S(1)}, bf16[18,64,128]{2,1,0:T(8,128)(2,1)S(1)}, u32[]{:S(2)}, u32[]{:S(2)}) collective-permute-start(bf16[18,64,128]{2,1,0:T(8,128)(2,1)S(1)} %get-tuple-element.39), channel_id=1, source_target_pairs={{4,0},{8,4},{12,8},{5,1},{9,5},{13,9},{6,2},{10,6},{14,10},{7,3},{... | collective-permute-start | bytes 884744 | tf_op jit(solution)/shard_map/ppermute | solution.py:29
  54.9 15.6 %copy-start.3 = (bf16[100,64,128]{2,1,0:T(8,128)(2,1)}, bf16[100,64,128]{2,1,0:T(8,128)(2,1)S(1)}, u32[]{:S(2)}) copy-start(bf16[100,64,128]{2,1,0:T(8,128)(2,1)S(1)} %fusion.6.refs_0_) | copy-start | bytes 4915204
  56.8 5.5 %copy-start.1 = (bf16[128,64,64]{1,0,2:T(8,128)(2,1)S(1)}, bf16[128,64,64]{1,0,2:T(8,128)(2,1)}, u32[]{:S(2)}) copy-start(bf16[128,64,64]{1,0,2:T(8,128)(2,1)} %copy.56) | copy-start | bytes 3145732
  56.9 9.5 %collective-permute-start.9 = (bf16[18,64,128]{2,1,0:T(8,128)(2,1)S(1)}, bf16[18,64,128]{2,1,0:T(8,128)(2,1)S(1)}, u32[]{:S(2)}, u32[]{:S(2)}) collective-permute-start(bf16[18,64,128]{2,1,0:T(8,128)(2,1)S(1)} %get-tuple-element.36), channel_id=1, source_target_pairs={{0,4},{4,8},{8,12},{1,5},{5,9},{9,13},{2,6},{6,10},{10,14},{3,7},{... | collective-permute-start | bytes 884744 | tf_op jit(solution)/shard_map/ppermute | solution.py:27
  59.1 9.3 %collective-permute-start.10 = (bf16[18,64,128]{2,1,0:T(8,128)(2,1)S(1)}, bf16[18,64,128]{2,1,0:T(8,128)(2,1)S(1)}, u32[]{:S(2)}, u32[]{:S(2)}) collective-permute-start(bf16[18,64,128]{2,1,0:T(8,128)(2,1)S(1)} %get-tuple-element.35), channel_id=1, source_target_pairs={{4,0},{8,4},{12,8},{5,1},{9,5},{13,9},{6,2},{10,6},{14,10},{7,3},{... | collective-permute-start | bytes 884744 | tf_op jit(solution)/shard_map/ppermute | solution.py:29
  63.1 7.4 %copy-start.12 = (s32[924]{0:T(1024)S(1)}, s32[924]{0:T(1024)}, u32[]{:S(2)}) copy-start(s32[924]{0:T(1024)} %concatenate.53.codes_ref) | copy-start | bytes 11092
  63.1 7.4 %copy-start.15 = (s32[32]{0:T(128)S(1)}, s32[32]{0:T(128)}, u32[]{:S(2)}) copy-start(s32[32]{0:T(128)} %get-tuple-element.19.groups_ref) | copy-start | bytes 388
  63.1 7.4 %copy-start.16 = (bf16[26,16,256]{2,1,0:T(8,128)(2,1)S(1)}, bf16[26,16,256]{2,1,0:T(8,128)(2,1)}, u32[]{:S(2)}) copy-start(bf16[26,16,256]{2,1,0:T(8,128)(2,1)} %constant.133.clone.factor_ref) | copy-start | bytes 638980
  63.1 7.4 %copy-start.18 = (bf16[26,16,256]{2,1,0:T(8,128)(2,1)S(1)}, bf16[26,16,256]{2,1,0:T(8,128)(2,1)}, u32[]{:S(2)}) copy-start(bf16[26,16,256]{2,1,0:T(8,128)(2,1)} %constant.134.clone.added_ref) | copy-start | bytes 638980
  63.2 45.7 %collective-permute-start.11 = (bf16[64,64,64]{2,1,0:T(8,128)(2,1)S(1)}, bf16[64,64,64]{2,1,0:T(8,128)(2,1)S(1)}, u32[]{:S(2)}, u32[]{:S(2)}) collective-permute-start(bf16[64,64,64]{2,1,0:T(8,128)(2,1)S(1)} %get-tuple-element.57), channel_id=1, source_target_pairs={{2,0},{0,2},{3,1},{1,3},{6,4},{4,6},{7,5},{5,7},{10,8},{8,10},{11,... | collective-permute-start | bytes 1572872 | tf_op jit(solution)/shard_map/ppermute | solution.py:39
  70.5 38.4 %copy-start.6 = (bf16[100,64,128]{2,1,0:T(8,128)(2,1)}, bf16[100,64,128]{2,1,0:T(8,128)(2,1)S(1)}, u32[]{:S(2)}) copy-start(bf16[100,64,128]{2,1,0:T(8,128)(2,1)S(1)} %fusion.3.refs_1_) | copy-start | bytes 4915204
  110.2 3.9 %copy-start.22 = (bf16[3,64,128]{2,1,0:T(8,128)(2,1)S(1)}, bf16[3,64,128]{2,1,0:T(8,128)(2,1)}, u32[]{:S(2)}) copy-start(bf16[3,64,128]{2,1,0:T(8,128)(2,1)} %param.16) | copy-start | bytes 147460
  110.2 11.2 %collective-permute-start.12 = (bf16[64,64,64]{2,1,0:T(8,128)(2,1)}, bf16[64,64,64]{2,1,0:T(8,128)(2,1)}, u32[]{:S(2)}, u32[]{:S(2)}) collective-permute-start(bf16[64,64,64]{2,1,0:T(8,128)(2,1)} %add_convert_fusion), channel_id=1, source_target_pairs={{1,0},{0,1},{3,2},{2,3},{5,4},{4,5},{7,6},{6,7},{9,8},{8,9},{11,10... | collective-permute-start | bytes 1572872 | tf_op jit(solution)/shard_map/ppermute | solution.py:39
  114.1 3.5 %collective-permute-start.13 = (bf16[8,64,64]{2,1,0:T(8,128)(2,1)}, bf16[8,64,64]{2,1,0:T(8,128)(2,1)}, u32[]{:S(2)}, u32[]{:S(2)}) collective-permute-start(bf16[8,64,64]{2,1,0:T(8,128)(2,1)} %convolution_convert_fusion), channel_id=1, source_target_pairs={{1,0},{0,1},{3,2},{2,3},{5,4},{4,5},{7,6},{6,7},{9,8},{8,9},{11,10... | collective-permute-start | bytes 196616 | tf_op jit(solution)/shard_map/ppermute | solution.py:39
  118.7 48.2 %collective-permute-start.14 = (bf16[16,64,64]{2,1,0:T(8,128)(2,1)S(1)}, bf16[16,64,64]{2,1,0:T(8,128)(2,1)S(1)}, u32[]{:S(2)}, u32[]{:S(2)}) collective-permute-start(bf16[16,64,64]{2,1,0:T(8,128)(2,1)S(1)} %pad_maximum_fusion.6), channel_id=1, source_target_pairs={{4,0},{8,4},{12,8},{0,12},{5,1},{9,5},{13,9},{1,13},{6,2},{10,6},{... | collective-permute-start | bytes 393224 | tf_op jit(solution)/shard_map/ppermute | solution.py:39
  120.1 46.8 %collective-permute-start.15 = (bf16[16,64,64]{2,1,0:T(8,128)(2,1)S(1)}, bf16[16,64,64]{2,1,0:T(8,128)(2,1)S(1)}, u32[]{:S(2)}, u32[]{:S(2)}) collective-permute-start(bf16[16,64,64]{2,1,0:T(8,128)(2,1)S(1)} %pad_maximum_fusion.6), channel_id=1, source_target_pairs={{8,0},{12,4},{0,8},{4,12},{9,1},{13,5},{1,9},{5,13},{10,2},{14,6},... | collective-permute-start | bytes 393224 | tf_op jit(solution)/shard_map/ppermute | solution.py:39
  120.1 46.8 %collective-permute-start.16 = (bf16[16,64,64]{2,1,0:T(8,128)(2,1)S(1)}, bf16[16,64,64]{2,1,0:T(8,128)(2,1)S(1)}, u32[]{:S(2)}, u32[]{:S(2)}) collective-permute-start(bf16[16,64,64]{2,1,0:T(8,128)(2,1)S(1)} %pad_maximum_fusion.6), channel_id=1, source_target_pairs={{12,0},{0,4},{4,8},{8,12},{13,1},{1,5},{5,9},{9,13},{14,2},{2,6},{... | collective-permute-start | bytes 393224 | tf_op jit(solution)/shard_map/ppermute | solution.py:39
  123.1 6.0 %copy-start.4 = (bf16[100,64,128]{2,1,0:T(8,128)(2,1)S(1)}, bf16[100,64,128]{2,1,0:T(8,128)(2,1)}, u32[]{:S(2)}) copy-start(bf16[100,64,128]{2,1,0:T(8,128)(2,1)} %copy-done.3) | copy-start | bytes 4915204
  123.1 6.0 %copy-start.7 = (bf16[100,64,128]{2,1,0:T(8,128)(2,1)S(1)}, bf16[100,64,128]{2,1,0:T(8,128)(2,1)}, u32[]{:S(2)}) copy-start(bf16[100,64,128]{2,1,0:T(8,128)(2,1)} %copy-done.6) | copy-start | bytes 4915204
  123.1 6.0 %copy-start.9 = (f32[32,3,128]{2,1,0:T(4,128)S(1)}, f32[32,3,128]{2,1,0:T(4,128)}, u32[]{:S(2)}) copy-start(f32[32,3,128]{2,1,0:T(4,128)} %get-tuple-element.45.own_ref) | copy-start | bytes 147460
  123.1 6.0 %copy-start.11 = (s32[924]{0:T(1024)S(1)}, s32[924]{0:T(1024)}, u32[]{:S(2)}) copy-start(s32[924]{0:T(1024)} %concatenate.50.codes_ref) | copy-start | bytes 11092
  123.1 6.0 %copy-start.14 = (s32[32]{0:T(128)S(1)}, s32[32]{0:T(128)}, u32[]{:S(2)}) copy-start(s32[32]{0:T(128)} %get-tuple-element.21.groups_ref) | copy-start | bytes 388
  123.1 6.0 %copy-start.17 = (bf16[26,16,256]{2,1,0:T(8,128)(2,1)S(1)}, bf16[26,16,256]{2,1,0:T(8,128)(2,1)}, u32[]{:S(2)}) copy-start(bf16[26,16,256]{2,1,0:T(8,128)(2,1)} %constant.133.clone.factor_ref) | copy-start | bytes 638980
  123.2 6.0 %copy-start.19 = (bf16[26,16,256]{2,1,0:T(8,128)(2,1)S(1)}, bf16[26,16,256]{2,1,0:T(8,128)(2,1)}, u32[]{:S(2)}) copy-start(bf16[26,16,256]{2,1,0:T(8,128)(2,1)} %constant.134.clone.added_ref) | copy-start | bytes 638980
  123.6 43.2 %collective-permute-start.17 = (bf16[47,64,64]{2,1,0:T(8,128)(2,1)S(1)}, bf16[47,64,64]{2,1,0:T(8,128)(2,1)S(1)}, u32[]{:S(2)}, u32[]{:S(2)}) collective-permute-start(bf16[47,64,64]{2,1,0:T(8,128)(2,1)S(1)} %slice.88), channel_id=1, source_target_pairs={{0,4},{4,8},{8,12},{1,5},{5,9},{9,13},{2,6},{6,10},{10,14},{3,7},{... | collective-permute-start | bytes 1155080 | tf_op jit(solution)/shard_map/ppermute | solution.py:27
  127.1 39.8 %collective-permute-start.18 = (bf16[47,64,64]{2,1,0:T(8,128)(2,1)S(1)}, bf16[47,64,64]{2,1,0:T(8,128)(2,1)S(1)}, u32[]{:S(2)}, u32[]{:S(2)}) collective-permute-start(bf16[47,64,64]{2,1,0:T(8,128)(2,1)S(1)} %slice.89), channel_id=1, source_target_pairs={{4,0},{8,4},{12,8},{5,1},{9,5},{13,9},{6,2},{10,6},{14,10},{7,3},{... | collective-permute-start | bytes 1155080 | tf_op jit(solution)/shard_map/ppermute | solution.py:29
  166.9 3.3 %copy-start.8 = (f32[64,3,64]{2,1,0:T(4,128)S(1)}, f32[64,3,64]{2,1,0:T(4,128)}, u32[]{:S(2)}) copy-start(f32[64,3,64]{2,1,0:T(4,128)} %maximum_convert_fusion.parent_skeleton_ref) | copy-start | bytes 147460
  202.6 3.6 %collective-permute-start.22 = (bf16[64,32,128]{2,1,0:T(8,128)(2,1)S(1)}, bf16[64,32,128]{2,1,0:T(8,128)(2,1)S(1)}, u32[]{:S(2)}, u32[]{:S(2)}) collective-permute-start(bf16[64,32,128]{2,1,0:T(8,128)(2,1)S(1)} %constant_dynamic-slice_fusion), channel_id=1, source_target_pairs={{1,0},{0,1},{3,2},{2,3},{5,4},{4,5},{7,6},{6,7},{9,8},{8,9},{11,10... | collective-permute-start | bytes 1572872 | tf_op jit(solution)/shard_map/ppermute | solution.py:39
  (4 other events, 5.7 us)
